TPU v7x, 32 devices: a whole 2x2x4 slice. The times are simulated.
32 devices in a mesh: dp: 8 (over y, x, core), mem: 4 (over z).
Axes of the slice: x: 2, y: 2, z: 4, core: 2. Of those that a mesh axis runs over, the one named last changes fastest.
Arguments:
- inputs: bfloat16 [32, 1024, 512], P(('dp', 'mem')), may hold values from -6 to 6
- memory: bfloat16 [32, 1024, 512], P('dp', 'mem'), may hold values from -6 to 6
- cotangent: bfloat16 [32, 1024, 512], P(('dp', 'mem')), may hold values from -6 to 6
- tgt_len: int32 [32, 16], P(('dp', 'mem')), may hold values from 0 to 1024, as said below
- src_len: int32 [32, 16], P('dp'), may hold values from 0 to 1024, as said below
- self_qkv: bfloat16 [512, 1536], replicated, may hold values from -0.25 to 0.25
- self_out: bfloat16 [512, 512], replicated, may hold values from -2 to 2
- cross_query: bfloat16 [512, 512], replicated, may hold values from -0.25 to 0.25
- cross_kv: bfloat16 [512, 1024], replicated, may hold values from -0.25 to 0.25
- cross_out: bfloat16 [512, 512], replicated, may hold values from -2 to 2
- ffn_in: bfloat16 [512, 2048], replicated, may hold values from -0.25 to 0.25
- ffn_out: bfloat16 [2048, 512], replicated, may hold values from -0.125 to 0.125
- ln_gain: float32 [3, 512], replicated, may hold values from 0.25 to 1.75
- ln_bias: float32 [3, 512], replicated, may hold values from -0.5 to 0.5
- omega_scale: float32 [3, 512], replicated, may hold values from 1 to 2.5
Outputs:
- output: bfloat16 [32, 1024, 512], P(('dp', 'mem'))
- input_grad: float32 [32, 1024, 512], P(('dp', 'mem'))
- memory_grad: float32 [32, 1024, 512], P('dp', 'mem')
- self_qkv_grad: float32 [512, 1536], replicated
- self_out_grad: float32 [512, 512], replicated
- cross_query_grad: float32 [512, 512], replicated
- cross_kv_grad: float32 [512, 1024], replicated
- cross_out_grad: float32 [512, 512], replicated
- ffn_in_grad: float32 [512, 2048], replicated
- ffn_out_grad: float32 [2048, 512], replicated
- ln_gain_grad: float32 [3, 512], replicated
- ln_bias_grad: float32 [3, 512], replicated
- omega_grad: float32 [3, 512], replicated
Inputs may be any that keep to these rules, and one draw needn't show every extreme that they name: A document row has its target length, at least 512, in column 0 and zeros elsewhere. A sentence row has 16 sentences of target length 1 to 64. Among the 4 rows of each dp index, one drawn from the seed is a document of target length 1024. The next row (cyclically) is a sentence row whose first sentence has target length 64. A row is of the same kind in tgt_len and src_len. `src_len`: A document row has its source length, at least 512, in column 0 and zeros elsewhere. A sentence row has 16 sources of length 1 to 64. The full-length document of each dp index has source length 1024. The sentence row after it has a first source of length 64.
All inputs are finite; a program needn't handle non-finite values.
Results may differ from a plain program's by a relative error of at most 0.02.
Values may be sent and summed in bfloat16 or wider, within the bound.
A program may use at most 192 MiB of HBM per device.

v0:
```python
import jax
import jax.numpy as jnp
from jax import lax
from jax.sharding import PartitionSpec as P

HEADS = 8
HEAD_DIM = 64
TGT_LEN = 1024
SRC_LEN = 1024
SENT = 64
SRC_SENT = 64


norm_eps = 1e-05
masked_fill = -1e30


def split_heads(values):
    return values.reshape(values.shape[0], HEADS, HEAD_DIM)


def layer_norm(values, gain_row, shift_row):
    centred = values - jnp.mean(values, axis=-1, keepdims=True)
    scaler = lax.rsqrt(jnp.mean(centred * centred, axis=-1, keepdims=True) + norm_eps)
    normed = centred * scaler
    return (normed * gain_row + shift_row, normed, scaler)


def norm_backward(upstream, normed, scaler, gain_row):
    scaled = upstream * gain_row
    centred = scaled - jnp.mean(scaled, axis=-1, keepdims=True)
    centred = centred - normed * jnp.mean(scaled * normed, axis=-1, keepdims=True)
    return (centred * scaler, jnp.sum(upstream * normed, axis=0), jnp.sum(upstream, axis=0))


def layout(positions, is_document, full_width, short_width, lengths):
    width = jnp.where(is_document, full_width, short_width).astype(jnp.int32)
    segment = positions // width
    offset = positions - segment * width
    slots = jnp.arange(lengths.shape[0], dtype=jnp.int32)
    bound = jnp.sum(jnp.where(segment[:, None] == slots[None, :], lengths[None, :], 0), axis=1)
    return (segment, offset < bound)


def block_scores(queries, key_rows, allowed):
    raw_scores = jnp.einsum(
        "qhd,khd->hqk",
        split_heads(queries),
        split_heads(key_rows),
        preferred_element_type=jnp.float32,
    )
    return jnp.where(allowed[None], raw_scores * HEAD_DIM ** (-0.5), masked_fill)


def causal_rule(target_row, is_document):

    def allowed(first_row, amount, key_count):
        query_pos = first_row + jnp.arange(amount, dtype=jnp.int32)
        key_pos = jnp.arange(key_count, dtype=jnp.int32)
        query_seg, _ = layout(query_pos, is_document, TGT_LEN, SENT, target_row)
        key_seg, key_valid = layout(key_pos, is_document, TGT_LEN, SENT, target_row)
        return (
            (key_pos[None, :] <= query_pos[:, None])
            & (query_seg[:, None] == key_seg[None, :])
            & key_valid[None, :]
        )

    return allowed


def source_rule(source_row, is_document, key_first, amount, key_count):
    query_pos = jnp.arange(amount, dtype=jnp.int32)
    key_pos = key_first + jnp.arange(key_count, dtype=jnp.int32)
    query_seg, _ = layout(query_pos, is_document, TGT_LEN, SENT, source_row)
    key_seg, key_valid = layout(key_pos, is_document, SRC_LEN, SRC_SENT, source_row)
    return (query_seg[:, None] == key_seg[None, :]) & key_valid[None, :]


def local_forward(queries, key_rows, value_rows, mask_rule):
    query_count = queries.shape[0]
    block_rows = min(512, query_count)

    def one_block(block_id):
        first_row = block_id * block_rows
        query_block = lax.dynamic_slice_in_dim(queries, first_row, block_rows, 0)
        scores = block_scores(
            query_block, key_rows, mask_rule(first_row, block_rows, key_rows.shape[0])
        )
        largest = jnp.max(scores, axis=-1, keepdims=True)
        exponent = jnp.exp(scores - largest)
        summed = jnp.sum(exponent, axis=-1, keepdims=True)
        weights = (exponent / summed).astype(jnp.bfloat16)
        mixed_rows = jnp.einsum(
            "hqk,khd->qhd", weights, split_heads(value_rows), preferred_element_type=jnp.float32
        )
        return (mixed_rows.reshape(block_rows, -1), largest[..., 0], summed[..., 0])

    mixed_rows, largest, summed = lax.map(
        one_block, jnp.arange(query_count // block_rows, dtype=jnp.int32)
    )
    return (mixed_rows.reshape(query_count, -1), largest, summed)


def local_backward(queries, key_rows, value_rows, mask_rule, largest, summed, upstream):
    block_rows = largest.shape[-1]
    key_heads = split_heads(key_rows)
    value_heads = split_heads(value_rows)
    key_count = key_rows.shape[0]

    def one_block(running, block_id):
        key_grad, value_grad = running
        first_row = block_id * block_rows
        query_block = lax.dynamic_slice_in_dim(queries, first_row, block_rows, 0)
        grad_heads = split_heads(lax.dynamic_slice_in_dim(upstream, first_row, block_rows, 0))
        scores = block_scores(query_block, key_rows, mask_rule(first_row, block_rows, key_count))
        weights = jnp.exp(scores - largest[block_id][..., None]) / summed[block_id][..., None]
        value_grad = value_grad + jnp.einsum(
            "hqk,qhd->khd",
            weights.astype(jnp.bfloat16),
            grad_heads,
            preferred_element_type=jnp.float32,
        )
        weight_grad = jnp.einsum(
            "qhd,khd->hqk", grad_heads, value_heads, preferred_element_type=jnp.float32
        )
        centre = jnp.sum(weight_grad * weights, axis=-1, keepdims=True)
        score_grad = (weights * (weight_grad - centre)).astype(jnp.bfloat16)
        query_grad = jnp.einsum(
            "hqk,khd->qhd", score_grad, key_heads, preferred_element_type=jnp.float32
        )
        key_grad = key_grad + jnp.einsum(
            "hqk,qhd->khd", score_grad, split_heads(query_block), preferred_element_type=jnp.float32
        )
        return ((key_grad, value_grad), query_grad.reshape(block_rows, -1) * HEAD_DIM ** (-0.5))

    zero_heads = jnp.zeros(key_heads.shape, jnp.float32)
    (key_grad, value_grad), query_grad = lax.scan(
        one_block, (zero_heads, zero_heads), jnp.arange(largest.shape[0], dtype=jnp.int32)
    )
    return (
        query_grad.reshape(queries.shape[0], -1),
        key_grad.reshape(key_count, -1) * HEAD_DIM ** (-0.5),
        value_grad.reshape(key_count, -1),
    )


def sweep_terms(
    query_one, kv_one, source_row, doc_one, key_first, largest_one, summed_one, grad_one
):
    model_dim = query_one.shape[-1]
    allowed = source_rule(source_row, doc_one, key_first, query_one.shape[0], kv_one.shape[0])
    scores = block_scores(query_one, kv_one[:, :model_dim], allowed)
    weights = jnp.exp(scores - largest_one[..., None]) / summed_one[..., None]
    weight_grad = jnp.einsum(
        "qhd,khd->hqk",
        split_heads(grad_one),
        split_heads(kv_one[:, model_dim:]),
        preferred_element_type=jnp.float32,
    )
    return (weights, weight_grad)


def per_device(
    inputs,
    memory,
    cotangent,
    tgt_len,
    src_len,
    self_qkv,
    self_out,
    cross_query,
    cross_kv,
    cross_out,
    ffn_in,
    ffn_out,
    ln_gain,
    ln_bias,
    omega_scale,
):
    seq_count, length, model_dim = inputs.shape
    group_count, piece_len, _ = memory.shape
    token_count = seq_count * length
    tokens = inputs.reshape(token_count, model_dim)
    tokens_f = tokens.astype(jnp.float32)
    encoded = memory.reshape(group_count * piece_len, model_dim)
    own_src = lax.dynamic_slice_in_dim(src_len, lax.axis_index("mem") * seq_count, seq_count, 0)
    own_doc = own_src[:, 0] > SRC_SENT
    group_doc = src_len[:, 0] > SRC_SENT
    places = jnp.arange(length, dtype=jnp.int32)
    keep_rows = jax.vmap(
        lambda target_row, doc_one: layout(places, doc_one, TGT_LEN, SENT, target_row)[1]
    )(tgt_len, own_doc).reshape(token_count, 1)
    packed = jnp.dot(tokens, self_qkv, preferred_element_type=jnp.float32).astype(jnp.bfloat16)
    packed_seq = packed.reshape(seq_count, length, 3 * model_dim)

    def self_forward(pieces):
        packed_one, target_row, doc_one = pieces
        return local_forward(
            packed_one[:, :model_dim],
            packed_one[:, model_dim : 2 * model_dim],
            packed_one[:, 2 * model_dim :],
            causal_rule(target_row, doc_one),
        )

    self_mixed, self_largest, self_summed = lax.map(self_forward, (packed_seq, tgt_len, own_doc))
    self_heads = self_mixed.reshape(token_count, model_dim).astype(jnp.bfloat16)
    branch = jnp.dot(self_heads, self_out, preferred_element_type=jnp.float32)
    first_out, first_normed, first_scaler = layer_norm(
        omega_scale[0] * tokens_f + branch, ln_gain[0], ln_bias[0]
    )
    first_low = first_out.astype(jnp.bfloat16)
    queries = (
        jnp.dot(first_low, cross_query, preferred_element_type=jnp.float32)
        .astype(jnp.bfloat16)
        .reshape(seq_count, length, model_dim)
    )
    memory_kv = (
        jnp.dot(encoded, cross_kv, preferred_element_type=jnp.float32)
        .astype(jnp.bfloat16)
        .reshape(group_count, piece_len, 2 * model_dim)
    )
    gathered = lax.all_gather(queries, "mem", axis=0, tiled=True)
    key_first = lax.axis_index("mem") * piece_len

    def stats_scores(pieces):
        query_one, kv_one, source_row, doc_one = pieces
        allowed = source_rule(source_row, doc_one, key_first, length, piece_len)
        return block_scores(query_one, kv_one[:, :model_dim], allowed)

    scores = lax.map(stats_scores, (gathered, memory_kv, src_len, group_doc))
    cross_largest = lax.pmax(jnp.max(scores, axis=-1).astype(jnp.bfloat16), "mem").astype(
        jnp.float32
    )
    exponent = jnp.exp(scores - cross_largest[..., None])
    cross_summed = lax.psum(jnp.sum(exponent, axis=-1), "mem")
    amount = seq_count * lax.axis_size("mem")
    kv_rows = memory_kv[..., model_dim:]
    weights = (exponent / cross_summed[..., None]).astype(jnp.bfloat16)
    mixed_rows = jnp.einsum(
        "ghqk,gkhd->gqhd",
        weights,
        kv_rows.reshape(amount, piece_len, HEADS, HEAD_DIM),
        preferred_element_type=jnp.float32,
    )
    cross_mixed = lax.psum_scatter(
        mixed_rows.reshape(amount, length, model_dim).astype(jnp.bfloat16),
        "mem",
        scatter_dimension=0,
        tiled=True,
    ).astype(jnp.float32)
    cross_heads = cross_mixed.reshape(token_count, model_dim).astype(jnp.bfloat16)
    branch = jnp.dot(cross_heads, cross_out, preferred_element_type=jnp.float32)
    second, second_normed, second_scaler = layer_norm(
        omega_scale[1] * first_out + branch, ln_gain[1], ln_bias[1]
    )
    second_low = second.astype(jnp.bfloat16)
    hidden = jnp.dot(second_low, ffn_in, preferred_element_type=jnp.float32)
    activation, gelu_back = jax.vjp(jax.nn.gelu, hidden)
    act_low = activation.astype(jnp.bfloat16)
    branch = jnp.dot(act_low, ffn_out, preferred_element_type=jnp.float32)
    third_out, third_normed, third_scaler = layer_norm(
        omega_scale[2] * second + branch, ln_gain[2], ln_bias[2]
    )
    result = jnp.where(keep_rows, third_out, 0.0)
    upstream = jnp.where(
        keep_rows, cotangent.reshape(token_count, model_dim).astype(jnp.float32), 0.0
    )
    pre_grad, gain_three, shift_three = norm_backward(
        upstream, third_normed, third_scaler, ln_gain[2]
    )
    scale_three = jnp.sum(pre_grad * second, axis=0)
    branch_grad = pre_grad.astype(jnp.bfloat16)
    out_weight_grad = jnp.einsum(
        "tf,td->fd", act_low, branch_grad, preferred_element_type=jnp.float32
    )
    act_grad = jnp.einsum("td,fd->tf", branch_grad, ffn_out, preferred_element_type=jnp.float32)
    hidden_grad = gelu_back(act_grad)[0].astype(jnp.bfloat16)
    in_weight_grad = jnp.einsum(
        "td,tf->df", second_low, hidden_grad, preferred_element_type=jnp.float32
    )
    second_grad = omega_scale[2] * pre_grad + jnp.einsum(
        "tf,df->td", hidden_grad, ffn_in, preferred_element_type=jnp.float32
    )
    pre_grad, gain_two, shift_two = norm_backward(
        second_grad, second_normed, second_scaler, ln_gain[1]
    )
    scale_two = jnp.sum(pre_grad * first_out, axis=0)
    branch_grad = pre_grad.astype(jnp.bfloat16)
    cross_out_weight = jnp.einsum(
        "td,te->de", cross_heads, branch_grad, preferred_element_type=jnp.float32
    )
    heads_grad = jnp.einsum(
        "te,de->td", branch_grad, cross_out, preferred_element_type=jnp.float32
    ).astype(jnp.bfloat16)
    heads_grad = heads_grad.reshape(seq_count, length, model_dim)
    grad_rows = lax.all_gather(heads_grad, "mem", axis=0, tiled=True)

    def first_sweep(pieces):
        query_one, kv_one, source_row, doc_one, largest_one, summed_one, grad_one = pieces
        weights, weight_grad = sweep_terms(
            query_one, kv_one, source_row, doc_one, key_first, largest_one, summed_one, grad_one
        )
        return jnp.sum(weight_grad * weights, axis=-1)

    sweep_inputs = (gathered, memory_kv, src_len, group_doc, cross_largest, cross_summed, grad_rows)
    centre = lax.psum(lax.map(first_sweep, sweep_inputs).astype(jnp.bfloat16), "mem").astype(
        jnp.float32
    )

    def second_sweep(pieces):
        query_one, kv_one, source_row, doc_one, largest_one, summed_one, grad_one, centre_one = (
            pieces
        )
        weights, weight_grad = sweep_terms(
            query_one, kv_one, source_row, doc_one, key_first, largest_one, summed_one, grad_one
        )
        grad_heads = split_heads(grad_one)
        value_grad = jnp.einsum(
            "hqk,qhd->khd",
            weights.astype(jnp.bfloat16),
            grad_heads,
            preferred_element_type=jnp.float32,
        )
        score_grad = (weights * (weight_grad - centre_one[..., None])).astype(jnp.bfloat16)
        query_grad = jnp.einsum(
            "hqk,khd->qhd",
            score_grad,
            split_heads(kv_one[:, :model_dim]),
            preferred_element_type=jnp.float32,
        ) * HEAD_DIM ** (-0.5)
        key_grad = jnp.einsum(
            "hqk,qhd->khd", score_grad, split_heads(query_one), preferred_element_type=jnp.float32
        ) * HEAD_DIM ** (-0.5)
        joined = jnp.concatenate(
            [key_grad.reshape(piece_len, -1), value_grad.reshape(piece_len, -1)], axis=-1
        )
        return (query_grad.reshape(length, -1), joined)

    query_parts, kv_grad_full = lax.map(second_sweep, sweep_inputs + (centre,))
    query_grad = lax.psum_scatter(
        query_parts.astype(jnp.bfloat16), "mem", scatter_dimension=0, tiled=True
    ).astype(jnp.float32)
    kv_grad = kv_grad_full.astype(jnp.bfloat16)
    query_low = query_grad.reshape(token_count, model_dim).astype(jnp.bfloat16)
    cross_query_weight = jnp.einsum(
        "td,te->de", first_low, query_low, preferred_element_type=jnp.float32
    )
    first_grad = omega_scale[1] * pre_grad + jnp.einsum(
        "te,de->td", query_low, cross_query, preferred_element_type=jnp.float32
    )
    kv_flat = kv_grad.reshape(group_count * piece_len, 2 * model_dim)
    memory_grad = jnp.einsum(
        "me,de->md", kv_flat, cross_kv, preferred_element_type=jnp.float32
    ).reshape(group_count, piece_len, model_dim)
    cross_kv_weight = jnp.einsum("md,me->de", encoded, kv_flat, preferred_element_type=jnp.float32)
    pre_grad, gain_one, shift_one = norm_backward(
        first_grad, first_normed, first_scaler, ln_gain[0]
    )
    scale_one = jnp.sum(pre_grad * tokens_f, axis=0)
    branch_grad = pre_grad.astype(jnp.bfloat16)
    self_out_weight = jnp.einsum(
        "td,te->de", self_heads, branch_grad, preferred_element_type=jnp.float32
    )
    heads_grad = jnp.einsum(
        "te,de->td", branch_grad, self_out, preferred_element_type=jnp.float32
    ).astype(jnp.bfloat16)
    heads_grad = heads_grad.reshape(seq_count, length, model_dim)

    def self_backward(pieces):
        packed_one, target_row, doc_one, largest_one, summed_one, grad_one = pieces
        return local_backward(
            packed_one[:, :model_dim],
            packed_one[:, model_dim : 2 * model_dim],
            packed_one[:, 2 * model_dim :],
            causal_rule(target_row, doc_one),
            largest_one,
            summed_one,
            grad_one,
        )

    query_grad, key_grad, value_grad = lax.map(
        self_backward, (packed_seq, tgt_len, own_doc, self_largest, self_summed, heads_grad)
    )
    packed_grad = (
        jnp.concatenate([query_grad, key_grad, value_grad], axis=-1)
        .astype(jnp.bfloat16)
        .reshape(token_count, 3 * model_dim)
    )
    self_qkv_weight = jnp.einsum(
        "td,te->de", tokens, packed_grad, preferred_element_type=jnp.float32
    )
    input_grad = omega_scale[0] * pre_grad + jnp.einsum(
        "te,de->td", packed_grad, self_qkv, preferred_element_type=jnp.float32
    )
    summed_all = lax.psum(
        (
            self_qkv_weight,
            self_out_weight,
            cross_query_weight,
            cross_kv_weight,
            cross_out_weight,
            in_weight_grad,
            out_weight_grad,
            gain_one,
            gain_two,
            gain_three,
            shift_one,
            shift_two,
            shift_three,
            scale_one,
            scale_two,
            scale_three,
        ),
        ("dp", "mem"),
    )
    (
        self_qkv_weight,
        self_out_weight,
        cross_query_weight,
        cross_kv_weight,
        cross_out_weight,
        in_weight_grad,
        out_weight_grad,
    ) = summed_all[:7]
    (
        gain_one,
        gain_two,
        gain_three,
        shift_one,
        shift_two,
        shift_three,
        scale_one,
        scale_two,
        scale_three,
    ) = summed_all[7:]
    gain_stack = jnp.stack([gain_one, gain_two, gain_three])
    shift_stack = jnp.stack([shift_one, shift_two, shift_three])
    scale_stack = jnp.stack([scale_one, scale_two, scale_three])
    return (
        result.reshape(seq_count, length, model_dim).astype(jnp.bfloat16),
        input_grad.reshape(seq_count, length, model_dim),
        memory_grad,
        self_qkv_weight,
        self_out_weight,
        cross_query_weight,
        cross_kv_weight,
        cross_out_weight,
        in_weight_grad,
        out_weight_grad,
        gain_stack,
        shift_stack,
        scale_stack,
    )


def solution(mesh):
    return jax.shard_map(
        per_device,
        mesh=mesh,
        in_specs=(
            P(("dp", "mem"), None, None),
            P("dp", "mem", None),
            P(("dp", "mem"), None, None),
            P(("dp", "mem"), None),
            P("dp", None),
            P(),
            P(),
            P(),
            P(),
            P(),
            P(),
            P(),
            P(),
            P(),
            P(),
        ),
        out_specs=(
            P(("dp", "mem"), None, None),
            P(("dp", "mem"), None, None),
            P("dp", "mem", None),
            P(),
            P(),
            P(),
            P(),
            P(),
            P(),
            P(),
            P(),
            P(),
            P(),
        ),
        check_vma=False,
    )
```

profile of v0, /device:TPU:0, one launch (start us, length us, event | category | flops | bytes accessed | tf_op | source)
XLA Modules:
  0.0 1192.1 jit_solution(11625032488309362741)
XLA Ops:
  24.9 38.5 %while.98 = (s32[]{:T(128)}, bf16[2,512,512]{2,1,0:T(8,128)(2,1)}, f32[2,8,512]{2,1,0:T(8,128)S(1)}, f32[2,8,512]{2,1,0:T(8,128)S(1)}, s32[2]{0:T(128)S(1)}, /*i...) while((s32[]{:T(128)}, bf16[2,512,512]{2,1,0:T(8,128)(2,1)}, ...), condition=%wide.region_5.6_spmd, body=%wide.region_1.5_spmd.sunk | while | flops 1126235136 | bytes 58898744 | solution.py:98
  77.8 75.2 %all-gather.5.cloned.1.call-done = bf16[4096,512]{1,0:T(8,128)(2,1)} async-done(((bf16[1024,512]{1,0:T(8,128)(2,1)}), bf16[4096,512]{1,0:T(8,128)(2,1)}) %all-gather.5.cloned.1.call-update) | async-done | bytes 4194320 | tf_op jit(solution)/shard_map/all_gather | solution.py:222
  153.0 6.2 copy.126
  159.2 36.2 %while.99 = (s32[]{:T(128)}, f32[4,8,1024,256]{3,2,1,0:T(8,128)}, pred[4]{0:T(512)(128)(4,1)S(1)}, s32[]{:T(128)}, s32[4,16]{1,0:T(4,128)S(1)}, /*index=5*/bf16[...) while((s32[]{:T(128)}, f32[4,8,1024,256]{3,2,1,0:T(8,128)}, ...), condition=%wide.region_10.11_spmd, body=%wide.region_8.10_spmd.sunk | while | flops 273179648 | bytes 13907832 | solution.py:230
  195.4 13.9 %reduce_max.22 = bf16[4,8,1024]{2,1,0:T(8,128)(2,1)} reduce(f32[4,8,1024,256]{3,2,1,0:T(8,128)} %get-tuple-element.889, bf16[]{:T(256)} %constant.584), dimensions={3}, to_apply=%region_11.12 | reduce | flops 8355840 | bytes 33619968 | tf_op jit(solution)/shard_map/reduce_max | solution.py:231
  209.4 32.6 %all-reduce.7.cloned.1.call-done = bf16[4,8,1024]{2,1,0:T(8,128)(2,1)} async-done(((bf16[4,8,1024]{2,1,0:T(8,128)(2,1)}), bf16[4,8,1024]{2,1,0:T(8,128)(2,1)}) %all-reduce.7.cloned.1.call-update) | async-done | bytes 65552 | tf_op jit(solution)/shard_map/pmax | solution.py:231
  242.9 16.0 %fusion.26 = f32[4,8,1024]{2,1,0:T(8,128)} fusion(f32[4,8,1024,256]{3,2,1,0:T(8,128)} %get-tuple-element.889, f32[4,8,1024]{2,1,0:T(8,128)S(1)} %convert_element_type.144), kind=kLoop, calls=%fused_computation.118 | loop fusion | flops 16744448 | bytes 33816576 | tf_op jit(solution)/shard_map/reduce_sum | solution.py:235
  261.6 31.7 %all-reduce.9.cloned.1.call-done = f32[4,8,1024]{2,1,0:T(8,128)} async-done(((f32[4,8,1024]{2,1,0:T(8,128)}), f32[4,8,1024]{2,1,0:T(8,128)}) %all-reduce.9.cloned.1.call-update) | async-done | bytes 131088 | tf_op jit(solution)/shard_map/psum | solution.py:235
  293.3 18.0 %fusion.35 = bf16[4,8,64,1024]{3,2,1,0:T(8,128)(2,1)} fusion(bf16[4,256,8,64]{1,3,2,0:T(8,128)(2,1)} %bitcast.395, f32[4,8,1024,256]{3,2,1,0:T(8,128)} %get-tuple-element.889, f32[4,8,1024]{2,1,0:T(8,128)} %all-reduce.9.cloned.1.call-done, f32[4,8,1024]{2,1,0:T(8,128)S(1)} %convert_element_type.144), kind=kOutput, calls=%fused_computation.133 | convolution fusion | flops 1101004800 | bytes 39059456 | tf_op jit(solution)/shard_map/ghqk,gkhd->gqhd/dot_general | solution.py:239
  313.4 74.5 %reduce-scatter.3.cloned.1.call-done = bf16[1,1024,512]{1,2,0:T(8,128)(2,1)} async-done(((bf16[4,1024,512]{1,2,0:T(8,128)(2,1)}), bf16[1,1024,512]{1,2,0:T(8,128)(2,1)}) %reduce-scatter.3.cloned.1.call-update) | async-done | bytes 1048592 | tf_op jit(solution)/shard_map/reduce_scatter | solution.py:245
  401.1 7.8 fusion.34
  419.0 81.4 %all-gather.7.cloned.1.call-done = bf16[4096,512]{1,0:T(8,128)(2,1)} async-done(((bf16[1024,512]{1,0:T(8,128)(2,1)}), bf16[4096,512]{1,0:T(8,128)(2,1)}) %all-gather.7.cloned.1.call-update) | async-done | bytes 4194320 | tf_op jit(solution)/shard_map/all_gather | solution.py:296
  500.3 6.7 copy.136
  507.1 59.8 %while.100 = (s32[]{:T(128)}, bf16[4,8,1024]{2,1,0:T(8,128)(2,1)S(1)}, bf16[4,1024,512]{1,2,0:T(8,128)(2,1)}, bf16[4,256,1024]{1,2,0:T(8,128)(2,1)}, pred[4]{0:T...) while((s32[]{:T(128)}, ...), condition=%wide.region_27.28_spmd, body=%wide.region_24.27_spmd.sunk | while | flops 549995520 | bytes 26474388 | solution.py:306
  567.6 32.6 %all-reduce.11.cloned.1.call-done = bf16[4,8,1024]{2,1,0:T(8,128)(2,1)} async-done(((bf16[4,8,1024]{2,1,0:T(8,128)(2,1)}), bf16[4,8,1024]{2,1,0:T(8,128)(2,1)}) %all-reduce.11.cloned.1.call-update) | async-done | bytes 65552 | tf_op jit(solution)/shard_map/psum | solution.py:306
  601.0 65.1 %while.101 = (s32[]{:T(128)}, bf16[4,1024,512]{1,2,0:T(8,128)(2,1)}, bf16[4,256,1024]{1,2,0:T(8,128)(2,1)}, bf16[4,256,1024]{1,2,0:T(8,128)(2,1)}, pred[4]{0:T(5...) while((s32[]{:T(128)}, bf16[4,1024,512]{1,2,0:T(8,128)(2,1)}, ...), condition=%wide.region_31.32_spmd, body=%wide.region_29.31_spmd.sunk | while | flops 1361863680 | bytes 54572972 | solution.py:339
  671.0 7.5 fusion.75
  678.6 6.5 fusion.68
  687.8 55.0 %reduce-scatter.5.cloned.1.call-done = bf16[1,1024,512]{1,2,0:T(8,128)(2,1)} async-done(((bf16[4,1024,512]{1,2,0:T(8,128)(2,1)}), bf16[1,1024,512]{1,2,0:T(8,128)(2,1)}) %reduce-scatter.5.cloned.1.call-update) | async-done | bytes 1048592 | tf_op jit(solution)/shard_map/reduce_scatter | solution.py:340
  753.4 117.1 %while.102 = (s32[]{:T(128)}, f32[1024,8,64]{0,2,1:T(8,128)}, f32[1024,8,64]{0,2,1:T(8,128)}, bf16[2,512,512]{2,1,0:T(8,128)(2,1)}, s32[2]{0:T(128)S(1)}, /*inde...) while((s32[]{:T(128)}, f32[1024,8,64]{0,2,1:T(8,128)}, ...), condition=%wide.region_38.39_spmd.clone, body=%wide.region_35.38_spmd.clone.sunk | while | flops 2731084288 | bytes 196770384 | solution.py:137
  758.0 8.4 exponential_divide_fusion.5
  766.7 10.9 multiply_reduce_fusion.16
  777.6 14.9 %multiply_convert_fusion.9 = bf16[8,512,1024]{2,1,0:T(8,128)(2,1)} fusion(f32[8,512,1024]{2,1,0:T(8,128)} %exponential_divide_fusion.5, f32[8,512,1024]{2,1,0:T(8,128)} %get-tuple-element.1783, f32[8,512]{1,0:T(8,128)S(1)} %get-tuple-element.1784), kind=kLoop, calls=%fused_computation.88.clone.1 | loop fusion | flops 12582912 | bytes 41959424 | tf_op jit(solution)/shard_map/while/body/eval_jaxpr/while/body/eval_jaxpr/convert_element_type | solution.py:127
  792.5 6.4 bitcast_add_fusion.4
  799.0 7.7 bitcast_add_fusion.5
  816.1 8.4 exponential_divide_fusion.5
  824.8 10.9 multiply_reduce_fusion.16
  835.8 14.9 %multiply_convert_fusion.9 = bf16[8,512,1024]{2,1,0:T(8,128)(2,1)} fusion(f32[8,512,1024]{2,1,0:T(8,128)} %exponential_divide_fusion.5, f32[8,512,1024]{2,1,0:T(8,128)} %get-tuple-element.1783, f32[8,512]{1,0:T(8,128)S(1)} %get-tuple-element.1784), kind=kLoop, calls=%fused_computation.88.clone.1 | loop fusion | flops 12582912 | bytes 41959424 | tf_op jit(solution)/shard_map/while/body/eval_jaxpr/while/body/eval_jaxpr/convert_element_type | solution.py:127
  850.7 7.0 bitcast_add_fusion.4
  857.7 7.7 bitcast_add_fusion.5
  896.4 42.8 %all-reduce = (f32[1,512]{1,0:T(1,128)S(1)}, f32[1,512]{1,0:T(1,128)S(1)}, f32[1,512]{1,0:T(1,128)S(1)}, f32[1,512]{1,0:T(1,128)S(1)}, f32[1,512]{1,0:T(1,128)S(...) all-reduce(f32[1,512]{1,0:T(1,128)S(1)} %bitcast.411, ...), channel_id=1, replica_groups=mesh['dp'=8,'mem'=4] {'dp','mem'}, use_global_device_ids=true, to_apply=%region_51.52 | all-reduce | flops 4608 | bytes 36864 | tf_op jit(solution)/shard_map/psum | solution.py:395
  941.0 227.9 %all-reduce.13.cloned.1.call-done = (f32[512,1536]{0,1:T(8,128)}, f32[512,512]{1,0:T(8,128)}, f32[512,512]{1,0:T(8,128)}, f32[512,1024]{0,1:T(8,128)}, f32[512,5...) async-done(((f32[512,1536]{0,1:T(8,128)}, f32[512,512]{1,0:T(8,128)}, f32[512,512]{1,0:T(8,128)}, f32[512,1024]{0,1:T(8,128)}, f32[512,512]{1,0:T(8,128)}, ...) | async-done | bytes 16777232 | tf_op jit(solution)/shard_map/psum | solution.py:395
  (555 shorter events, 326.9 us)
Async XLA Ops:
  7.2 388.8 %copy-start = (bf16[2048,512]{1,0:T(8,128)(2,1)S(1)}, bf16[2048,512]{1,0:T(8,128)(2,1)}, u32[]{:S(2)}) copy-start(bf16[2048,512]{1,0:T(8,128)(2,1)} %param.36) | copy-start | bytes 6291460
  7.2 145.8 %all-gather.5.cloned.1.call-start = ((), (), s32[]{:S(2)}) async-start(), calls=%async_computation.7 | async-start | bytes 5242880 | tf_op jit(solution)/shard_map/all_gather | solution.py:222
  24.9 38.5 %copy-start.83 = (f32[3,512]{1,0:T(4,128)S(1)}, f32[3,512]{1,0:T(4,128)}, u32[]{:S(2)}) copy-start(f32[3,512]{1,0:T(4,128)} %param.39) | copy-start | bytes 18436
  63.4 324.5 %copy-start.91 = (f32[1,512]{1,0:T(1,128)}, f32[1,512]{1,0:T(1,128)S(1)}, u32[]{:S(2)}) copy-start(f32[1,512]{1,0:T(1,128)S(1)} %get-tuple-element.1394) | copy-start | bytes 6148
  66.0 321.9 %copy-start.53 = (f32[1024]{0:T(1024)}, f32[1024]{0:T(1024)S(1)}, u32[]{:S(2)}) copy-start(f32[1024]{0:T(1024)S(1)} %broadcast_multiply_fusion.8) | copy-start | bytes 12292
  66.3 321.6 %copy-start.64 = (f32[1024]{0:T(1024)}, f32[1024]{0:T(1024)S(1)}, u32[]{:S(2)}) copy-start(f32[1024]{0:T(1024)S(1)} %add_rsqrt_fusion.2) | copy-start | bytes 12292
  69.4 172.7 %all-reduce.7.cloned.1.call-start = ((), (), s32[]{:S(2)}) async-start(), calls=%async_computation.2 | async-start | bytes 131072 | tf_op jit(solution)/shard_map/pmax | solution.py:231
  209.3 83.9 %all-reduce.9.cloned.1.call-start = ((), (), s32[]{:S(2)}) async-start(), calls=%async_computation.3 | async-start | bytes 262144 | tf_op jit(solution)/shard_map/psum | solution.py:235
  258.9 128.9 %reduce-scatter.3.cloned.1.call-start = ((), (), s32[]{:S(2)}) async-start(), calls=%async_computation.4 | async-start | bytes 5242880 | tf_op jit(solution)/shard_map/reduce_scatter | solution.py:245
  311.3 189.0 %all-gather.7.cloned.1.call-start = ((), (), s32[]{:S(2)}) async-start(), calls=%async_computation.8 | async-start | bytes 5242880 | tf_op jit(solution)/shard_map/all_gather | solution.py:296
  313.0 98.8 %copy-start.20 = (bf16[1,1024,512]{1,2,0:T(8,128)(2,1)}, bf16[1,1024,512]{1,2,0:T(8,128)(2,1)S(1)}, u32[]{:S(2)}) copy-start(bf16[1,1024,512]{1,2,0:T(8,128)(2,1)S(1)} %copy.129) | copy-start | bytes 3145732
  313.4 98.4 %copy-start.67 = (pred[1024]{0:T(1024)(128)(4,1)}, pred[1024]{0:T(1024)(128)(4,1)S(1)}, u32[]{:S(2)}) copy-start(pred[1024]{0:T(1024)(128)(4,1)S(1)} %subtract_compare_fusion.5) | copy-start | bytes 3076
  391.0 25.1 %copy-start.11 = (f32[1024,512]{0,1:T(8,128)}, f32[1024,512]{0,1:T(8,128)S(1)}, u32[]{:S(2)}) copy-start(f32[1024,512]{0,1:T(8,128)S(1)} %get-tuple-element.1400) | copy-start | bytes 6291460
  391.0 25.1 %copy-start.44 = (f32[1024]{0:T(1024)}, f32[1024]{0:T(1024)S(1)}, u32[]{:S(2)}) copy-start(f32[1024]{0:T(1024)S(1)} %broadcast_multiply_fusion.7) | copy-start | bytes 12292
  391.3 24.7 %copy-start.51 = (f32[1024]{0:T(1024)}, f32[1024]{0:T(1024)S(1)}, u32[]{:S(2)}) copy-start(f32[1024]{0:T(1024)S(1)} %add_rsqrt_fusion.1) | copy-start | bytes 12292
  399.8 12.0 %copy-start.13 = (f32[1024,512]{0,1:T(8,128)}, f32[1024,512]{0,1:T(8,128)S(1)}, u32[]{:S(2)}) copy-start(f32[1024,512]{0,1:T(8,128)S(1)} %get-tuple-element.1402) | copy-start | bytes 6291460
  399.8 12.0 %copy-start.42 = (f32[1024]{0:T(1024)}, f32[1024]{0:T(1024)S(1)}, u32[]{:S(2)}) copy-start(f32[1024]{0:T(1024)S(1)} %broadcast_multiply_fusion.6) | copy-start | bytes 12292
  400.1 11.7 copy-start.49
  401.1 10.8 copy-start.60
  401.1 10.8 copy-start.62
  418.9 181.3 %all-reduce.11.cloned.1.call-start = ((), (), s32[]{:S(2)}) async-start(), calls=%async_computation.5 | async-start | bytes 131072 | tf_op jit(solution)/shard_map/psum | solution.py:306
  567.5 175.3 %reduce-scatter.5.cloned.1.call-start = ((), (), s32[]{:S(2)}) async-start(), calls=%async_computation.6 | async-start | bytes 5242880 | tf_op jit(solution)/shard_map/reduce_scatter | solution.py:340
  666.2 502.7 %all-reduce.13.cloned.1.call-start = ((), (), s32[]{:S(2)}) async-start(), calls=%async_computation.9 | async-start | bytes 33554432 | tf_op jit(solution)/shard_map/psum | solution.py:395
  685.1 57.7 %copy-start.9 = (f32[1024,512]{0,1:T(8,128)S(1)}, f32[1024,512]{0,1:T(8,128)}, u32[]{:S(2)}) copy-start(f32[1024,512]{0,1:T(8,128)} %copy-done.8) | copy-start | bytes 6291460
  685.1 57.7 %copy-start.54 = (f32[1024]{0:T(1024)S(1)}, f32[1024]{0:T(1024)}, u32[]{:S(2)}) copy-start(f32[1024]{0:T(1024)} %copy-done.53) | copy-start | bytes 12292
  685.1 57.7 %copy-start.65 = (f32[1024]{0:T(1024)S(1)}, f32[1024]{0:T(1024)}, u32[]{:S(2)}) copy-start(f32[1024]{0:T(1024)} %copy-done.64) | copy-start | bytes 12292
  685.2 57.7 %copy-start.78 = (f32[1,512]{1,0:T(1,128)S(1)}, f32[1,512]{1,0:T(1,128)}, u32[]{:S(2)}) copy-start(f32[1,512]{1,0:T(1,128)} %get-tuple-element.1389) | copy-start | bytes 6148
  685.2 57.7 %copy-start.89 = (f32[1,512]{1,0:T(1,128)S(1)}, f32[1,512]{1,0:T(1,128)}, u32[]{:S(2)}) copy-start(f32[1,512]{1,0:T(1,128)} %get-tuple-element.1392) | copy-start | bytes 6148
  685.2 57.7 %copy-start.92 = (f32[1,512]{1,0:T(1,128)S(1)}, f32[1,512]{1,0:T(1,128)}, u32[]{:S(2)}) copy-start(f32[1,512]{1,0:T(1,128)} %copy-done.91) | copy-start | bytes 6148
  687.8 59.2 %copy-start.19 = (bf16[1,1024,512]{1,2,0:T(8,128)(2,1)S(1)}, bf16[1,1024,512]{1,2,0:T(8,128)(2,1)}, u32[]{:S(2)}) copy-start(bf16[1,1024,512]{1,2,0:T(8,128)(2,1)} %copy.120) | copy-start | bytes 3145732
  792.5 15.5 %slice-start = ((s8[8388608]{0:T(1024)(128)(4,1)}), s8[4194304]{0:T(1024)(128)(4,1)S(1)}, s32[]{:S(2)}) async-start(s8[8388608]{0:T(1024)(128)(4,1)} %bitcast.355), calls=%async_computation.10 | async-start | bytes 8388608 | tf_op jit(solution)/shard_map/while/body/eval_jaxpr/while
  850.7 16.1 %slice-start = ((s8[8388608]{0:T(1024)(128)(4,1)}), s8[4194304]{0:T(1024)(128)(4,1)S(1)}, s32[]{:S(2)}) async-start(s8[8388608]{0:T(1024)(128)(4,1)} %bitcast.355), calls=%async_computation.10 | async-start | bytes 8388608 | tf_op jit(solution)/shard_map/while/body/eval_jaxpr/while
  (88 other events, 360.2 us)
Sparse Core Ops, SparseCore 0:
  69.5 83.4 all-gather.4
  209.5 32.5 all-reduce.6
  259.1 34.1 all-reduce.8
  311.4 76.3 reduce-scatter.2
  419.0 81.2 all-gather.6
  567.6 32.5 all-reduce.10
  666.3 76.4 reduce-scatter.4
  883.4 285.4 all-reduce.12
where the time goes:
time: 1200 us; the launch traced here: 1190 us
  waiting for transfers between devices  611 us (51%)
  matrix products  285 us (24%)
  local copies, waits for them, and re-layouts  122 us (10%)
  other arithmetic  98.3 us (8%)
  blocking collectives  42.8 us (4%)
  between operations  15.8 us (1%)
  loops' own time  15.6 us (1%)
    psum x1, waiting for transfers between devices, per_device(): lax.psum((self_qkv_weight, self_out_weight, cross_query_weight, cross_kv_...  228 us
    dot_general x16, matrix products, block_scores(): jnp.einsum('qhd,khd->hqk', split_heads(queries), split_heads(key_rows), p...  84.1 us
    all_gather x1, waiting for transfers between devices, per_device(): grad_rows = lax.all_gather(heads_grad, 'mem', axis=0, tiled=True)  81.4 us
    all_gather x1, waiting for transfers between devices, per_device(): gathered = lax.all_gather(queries, 'mem', axis=0, tiled=True)  75.2 us
    reduce_scatter x1, waiting for transfers between devices, per_device(): lax.psum_scatter(mixed_rows.reshape(amount, length, model_dim).astype(jnp...  74.5 us
    reduce_scatter x1, waiting for transfers between devices, per_device(): lax.psum_scatter(query_parts.astype(jnp.bfloat16), 'mem', scatter_dimensi...  55 us
    psum x1, blocking collectives, per_device(): lax.psum((self_qkv_weight, self_out_weight, cross_query_weight, cross_kv_...  42.8 us
    pmax x1, waiting for transfers between devices, per_device(): lax.pmax(jnp.max(scores, axis=-1).astype(jnp.bfloat16), 'mem')  32.6 us
  transfers between devices with their start and end apart: 8, of which 8 were waited for; matrix products, arithmetic and copies ran while one was open for 4% of the time, Pallas kernels for 0%

commit v1 on v0

v1 whole, which is shorter than its diff:
```python
import functools

import jax
import jax.numpy as jnp
from jax import lax
from jax.experimental import pallas as pl
from jax.experimental.pallas import tpu as pltpu
from jax.sharding import PartitionSpec as P

f32 = jnp.float32
bf = jnp.bfloat16
MESH = pl.DeviceIdType.MESH
NN = (((1,), (0,)), ((), ()))
NT = (((1,), (1,)), ((), ()))
TN = (((0,), (0,)), ((), ()))

L = 1024
D = 512
FF = 2048
HEADS = 8
PAIRS = HEADS // 2
SHORT = 64
SCALE = 0.125
NEG = -1e30
EPS = 1e-05
GELU_C = 0.7978845608028654
GELU_A = 0.044715


def dot(a, b, dims=NN):
    return lax.dot_general(a, b, dims, preferred_element_type=f32)


def span(i, n):
    return pl.ds(pl.multiple_of(i * n, n), n)


def loop(n, body):
    def step(i, carry):
        body(i)
        return carry

    lax.fori_loop(0, n, step, 0)


def half_lanes():
    return lax.broadcasted_iota(jnp.int32, (1, 128), 1) < 64


def norm(values):
    centred = values - jnp.mean(values, axis=-1, keepdims=True)
    scaler = lax.rsqrt(jnp.mean(centred * centred, axis=-1, keepdims=True) + EPS)
    return centred * scaler, scaler


def norm_back(upstream, normed, scaler, gain_row):
    scaled = upstream * gain_row
    centred = scaled - jnp.mean(scaled, axis=-1, keepdims=True)
    centred = centred - normed * jnp.mean(scaled * normed, axis=-1, keepdims=True)
    return centred * scaler


def total(values):
    return jnp.sum(values, axis=0, keepdims=True)


def three_parts(values, base):
    lane = lax.broadcasted_iota(jnp.int32, (1, 128), 1)
    high = values.astype(bf).astype(f32)
    rest = values - high
    middle = rest.astype(bf).astype(f32)
    low = rest - middle
    picked = jnp.where(lane == 16, high, jnp.where(lane == 17, middle, jnp.where(lane == 18, low, base)))
    return picked.astype(bf)


def key_features(lengths, is_doc, rows, first):
    pos = first + lax.broadcasted_iota(jnp.int32, (rows, 128), 0)
    lane = lax.broadcasted_iota(jnp.int32, (rows, 128), 1)
    seg = (pos >> 6) * (1 - is_doc)
    inside = (seg == lane) & (pos - seg * SHORT < lengths)
    feats = jnp.where(lane < 16, jnp.where(inside, 0.0, NEG), jnp.where(lane < 19, 1.0, 0.0))
    hot = jnp.where(seg == lane, 1.0, 0.0)
    return feats.astype(bf), hot.astype(bf), jnp.where(inside, 1.0, 0.0)


def softmax_pair(qp, sections, heads, lse_out, base):
    half = half_lanes()
    mixed = []
    for e in range(2):
        sel = half if e == 0 else jnp.logical_not(half)
        qa = jnp.concatenate([jnp.where(sel, qp, jnp.zeros_like(qp)), base], axis=1)
        scores = []
        largest = None
        for keys, _, mask in sections:
            s = dot(qa, keys, NT)
            if mask is not None:
                s = jnp.where(mask, s, NEG)
            scores.append(s)
            m = jnp.max(s, axis=1, keepdims=True)
            largest = m if largest is None else jnp.maximum(largest, m)
        acc = None
        for s, (_, values, _) in zip(scores, sections):
            o = dot(jnp.exp(s - largest).astype(bf), values)
            acc = o if acc is None else acc + o
        summed = acc[:, 128:]
        lse_out(e, three_parts(-(largest + jnp.log(summed)), base.astype(f32)))
        mixed.append(acc[:, :128] / summed)
    heads(jnp.where(half, mixed[0], mixed[1]).astype(bf))


def back_tile(ka, va, k_rows, qp, qfeat, gp, gfeat, mask):
    half = half_lanes()
    dk, dv, dq = [], [], []
    for e in range(2):
        sel = half if e == 0 else jnp.logical_not(half)
        qa = jnp.concatenate([jnp.where(sel, qp, jnp.zeros_like(qp)), qfeat[e]], axis=1)
        ga = jnp.concatenate([jnp.where(sel, gp, jnp.zeros_like(gp)), gfeat[e]], axis=1)
        probs = jnp.exp(dot(ka, qa, NT))
        if mask is not None:
            width = mask.shape[1]
            first = jnp.where(mask, probs[:, :width], 0.0)
            probs = first if probs.shape[1] == width else jnp.concatenate([first, probs[:, width:]], axis=1)
        ds = (probs * dot(va, ga, NT)).astype(bf)
        dv.append(dot(probs.astype(bf), gp))
        dk.append(dot(ds, qp))
        dq.append(dot(ds, k_rows, TN))
    return (
        jnp.where(half, dk[0], dk[1]),
        jnp.where(half, dv[0], dv[1]),
        jnp.where(half, dq[0], dq[1]),
    )


def delta_features(product, store):
    half = half_lanes()
    for j in range(PAIRS):
        part = product[:, 128 * j : 128 * (j + 1)]
        for e in range(2):
            sel = half if e == 0 else jnp.logical_not(half)
            delta = jnp.sum(jnp.where(sel, part, 0.0), axis=1, keepdims=True)
            store(2 * j + e, three_parts(jnp.broadcast_to(-delta, part.shape), jnp.zeros_like(part)))


SELF_BQ = 256
SELF_BK = 256
CROSS_BQ = 512
CROSS_BK = 256
TB = 256


def forward_kernel(
    x, meml, cot, meta, wqkv, wso, wcq, wckv, wco, win, wout, gain, bias, omega,
    out, packed, sh, qfs, kfs, n1, r1, q8, mem, kv, qfc, kfc, dfc, pre2, do, gffn, vecs,
    hot, keep, ch, act, hg, br3, slow, br2, dg, send_sem, recv_sem, own_sem,
):
    me = lax.axis_index("mem")
    dp = lax.axis_index("dp")
    n = 4
    piece = L // n
    barrier = pltpu.get_barrier_semaphore()
    for t in range(1, n):
        pl.semaphore_signal(barrier, inc=1, device_id=(dp, lax.rem(me + t, n)), device_id_type=MESH)
    pl.semaphore_wait(barrier, n - 1)

    def exchange(t):
        peer = lax.rem(me + t, n)
        return pltpu.make_async_remote_copy(
            src_ref=meml.at[peer],
            dst_ref=mem.at[span(me, piece), :],
            send_sem=send_sem.at[t],
            recv_sem=recv_sem.at[t],
            device_id=(dp, peer),
            device_id_type=MESH,
        )

    own = pltpu.make_async_copy(meml.at[me], mem.at[span(me, piece), :], own_sem)
    for t in range(1, n):
        exchange(t).start()
    own.start()

    is_doc = (meta[1:2, 0:1] > SHORT).astype(jnp.int32)

    def features(i):
        rows = span(i, TB)
        feats, one_hot, inside = key_features(meta[0:1, :], is_doc, TB, i * TB)
        kfs[rows, :] = feats
        hot[rows, :] = one_hot
        keep[rows, :] = jnp.sum(inside, axis=1, keepdims=True)
        feats, _, _ = key_features(meta[1:2, :], is_doc, TB, i * TB)
        kfc[rows, :] = feats

    loop(L // TB, features)

    def project(i):
        rows = span(i, TB)
        packed[rows, :D] = dot(x[rows, :], wqkv[:, :D]).astype(bf) * bf(SCALE)
        packed[rows, D:] = dot(x[rows, :], wqkv[:, D:]).astype(bf)

    loop(L // TB, project)

    ones = jnp.ones((SELF_BQ, 128), bf)
    causal = lax.broadcasted_iota(jnp.int32, (SELF_BQ, SELF_BQ), 0) >= lax.broadcasted_iota(
        jnp.int32, (SELF_BQ, SELF_BQ), 1
    )
    for b in range(L // SELF_BQ):
        low, high = b * SELF_BQ, (b + 1) * SELF_BQ

        def self_pair(j, low=low, high=high):
            def section(first, last, mask):
                return (
                    jnp.concatenate([packed[first:last, pl.ds(pl.multiple_of(D + j * 128, 128), 128)], kfs[first:last, :]], axis=1),
                    jnp.concatenate([packed[first:last, pl.ds(pl.multiple_of(2 * D + j * 128, 128), 128)], jnp.ones((last - first, 128), bf)], axis=1),
                    mask,
                )

            sections = [section(low, high, causal)]
            if low:
                sections.append(section(0, low, None))

            def heads(value):
                sh[low:high, span(j, 128)] = value

            def lse_out(e, value):
                qfs[2 * j + e, low:high, :] = value

            softmax_pair(packed[low:high, span(j, 128)], sections, heads, lse_out, hot[low:high, :])

        loop(PAIRS, self_pair)

    def first_norm(i):
        rows = span(i, TB)
        normed, scaler = norm(omega[0:1, :] * x[rows, :].astype(f32) + dot(sh[rows, :], wso[...]))
        n1[rows, :] = normed
        r1[rows, :] = scaler
        first = (normed * gain[0:1, :] + bias[0:1, :]).astype(bf)
        q8[rows, :] = dot(first, wcq[...]).astype(bf) * bf(SCALE)

    loop(L // TB, first_norm)

    own.wait()
    for t in range(1, n):
        exchange(t).wait()

    def memory_project(i):
        rows = span(i, TB)
        kv[rows, :] = dot(mem[rows, :], wckv[...]).astype(bf)

    loop(L // TB, memory_project)

    def cross_pair(i):
        j = i // (L // CROSS_BQ)
        rows = span(lax.rem(i, L // CROSS_BQ), CROSS_BQ)
        keys = jnp.concatenate([kv[:, span(j, 128)], kfc[...]], axis=1)
        values = jnp.concatenate(
            [kv[:, pl.ds(pl.multiple_of(D + j * 128, 128), 128)], jnp.ones((L, 128), bf)], axis=1
        )

        def heads(value):
            ch[rows, span(j, 128)] = value

        def lse_out(e, value):
            qfc[2 * j + e, rows, :] = value

        softmax_pair(q8[rows, span(j, 128)], [(keys, values, None)], heads, lse_out, hot[rows, :])

    loop(PAIRS * (L // CROSS_BQ), cross_pair)

    vecs[...] = jnp.zeros_like(vecs)
    wide = 512

    def tokens(i):
        rows = span(i, TB)
        first = n1[rows, :] * gain[0:1, :] + bias[0:1, :]
        n2, r2 = norm(omega[1:2, :] * first + dot(ch[rows, :], wco[...]))
        second = n2 * gain[1:2, :] + bias[1:2, :]
        second_low = second.astype(bf)
        slow[rows, :] = second_low
        branch = jnp.zeros((TB, D), f32)
        for c in range(FF // wide):
            cols = slice(c * wide, (c + 1) * wide)
            h = dot(second_low, win[:, cols])
            square = h * h
            th = jnp.tanh(GELU_C * (h + GELU_A * (h * square)))
            cdf = 0.5 * (1.0 + th)
            low = (h * cdf).astype(bf)
            act[rows, cols] = low
            dg[:, cols] = cdf + 0.5 * h * (1.0 - th * th) * (GELU_C * (1.0 + 3.0 * GELU_A * square))
            branch = branch + dot(low, wout[cols, :])
        n3, r3 = norm(omega[2:3, :] * second + branch)
        third = n3 * gain[2:3, :] + bias[2:3, :]
        kept = keep[rows, :]
        out[rows, :] = (third * kept).astype(bf)
        up = cot[rows, :].astype(f32) * kept
        pre3 = norm_back(up, n3, r3, gain[2:3, :])
        vecs[2:3, :] += total(up * n3)
        vecs[5:6, :] += total(up)
        vecs[8:9, :] += total(pre3 * second)
        low3 = pre3.astype(bf)
        br3[rows, :] = low3
        grad = omega[2:3, :] * pre3
        for c in range(FF // wide):
            cols = slice(c * wide, (c + 1) * wide)
            hl = (dot(low3, wout[cols, :], NT) * dg[:, cols]).astype(bf)
            hg[rows, cols] = hl
            grad = grad + dot(hl, win[:, cols], NT)
        back2 = norm_back(grad, n2, r2, gain[1:2, :])
        vecs[1:2, :] += total(grad * n2)
        vecs[4:5, :] += total(grad)
        vecs[7:8, :] += total(back2 * first)
        pre2[rows, :] = back2
        low2 = back2.astype(bf)
        br2[rows, :] = low2
        dlow = dot(low2, wco[...], NT).astype(bf)
        do[rows, :] = dlow

        def store(h, value):
            dfc[h, rows, :] = value

        delta_features(dlow.astype(f32) * ch[rows, :].astype(f32), store)

    loop(L // TB, tokens)

    def out_weight(i):
        gffn[span(i, 256), :] = dot(act[:, span(i, 256)], br3[...], TN).astype(bf)

    loop(FF // 256, out_weight)
    for c in range(FF // wide):

        def in_weight(i, c=c):
            gffn[pl.ds(pl.multiple_of(FF + c * 512 + i * 256, 256), 256), :] = dot(
                slow[:, span(i, 256)], hg[:, c * wide : (c + 1) * wide], TN
            ).astype(bf)

        loop(2, in_weight)

    def cross_out_weight(i):
        gffn[pl.ds(pl.multiple_of(2 * FF + i * 256, 256), 256), :] = dot(
            ch[:, span(i, 256)], br2[...], TN
        ).astype(bf)

    loop(2, cross_out_weight)


class Segment:
    def __init__(self, index, source, base, n, parts, acc, bufs, fin, final, final_base, sems, place):
        self.index, self.source, self.base, self.n, self.parts = index, source, base, n, parts
        self.acc, (self.r0, self.r1, self.r2, self.r3), self.fin = acc, bufs, fin
        self.final, self.final_base = final, final_base
        self.send, self.recv, self.local = sems
        self.place = place

    def rows(self, first, count):
        return pl.ds(pl.multiple_of(first, 16), count)

    def remote(self, src, dst, k, device):
        return pltpu.make_async_remote_copy(
            src_ref=src,
            dst_ref=dst,
            send_sem=self.send.at[self.index, k],
            recv_sem=self.recv.at[self.index, k],
            device_id=device,
            device_id_type=MESH,
        )

    def core_copy(self):
        n, (dp, me, bits) = self.n, self.place
        other = 1 - bits[0]
        return self.remote(
            self.source.at[self.rows(self.base + other * (n // 2), n // 2), :],
            self.r0,
            0,
            (dp + 1 - 2 * bits[0], me),
        )

    def own_copy(self):
        n, (_, _, bits) = self.n, self.place
        return pltpu.make_async_copy(
            self.source.at[self.rows(self.base + bits[0] * (n // 2), n // 2), :],
            self.acc,
            self.local.at[self.index],
        )

    def partner(self, axis):
        dp, me, bits = self.place
        return (dp + 2 * axis * (1 - 2 * bits[axis]), me)

    def axes(self, p):
        return (1, 2) if self.parts[p][2] == 0 else (2, 1)

    def lanes(self, p):
        return slice(self.parts[p][0], self.parts[p][1])

    def offset(self, p, depth):
        if depth == 0:
            return 0
        n, (_, me, bits) = self.n, self.place
        one, two = self.axes(p)
        result = bits[one] * (n // 4)
        if depth > 1:
            result = result + bits[two] * (n // 8)
        if depth > 2:
            result = result + me * (n // 32)
        return result

    def halving(self, p, depth):
        n, (_, _, bits) = self.n, self.place
        axis = self.axes(p)[depth - 1]
        size = n // (4 if depth == 1 else 8)
        other = self.offset(p, depth - 1) + (1 - bits[axis]) * size
        buf = self.r1 if depth == 1 else self.r2
        return self.remote(
            self.acc.at[self.rows(other, size), self.lanes(p)],
            buf.at[:, self.lanes(p)],
            2 * depth - 1 + p,
            self.partner(axis),
        )

    def quarter(self, p, t):
        n, (dp, me, _) = self.n, self.place
        peer = lax.rem(me + t, 4)
        return self.remote(
            self.acc.at[self.rows(self.offset(p, 2) + peer * (n // 32), n // 32), self.lanes(p)],
            self.r3.at[t - 1, :, self.lanes(p)],
            5 + 3 * p + t - 1,
            (dp, peer),
        )

    def final_rows(self, p, depth):
        n, (_, _, bits) = self.n, self.place
        size = n // (2, 4, 8, 32)[depth]
        return self.final.at[
            self.rows(self.final_base + bits[0] * (n // 2) + self.offset(p, depth), size),
            slice(None) if p is None else self.lanes(p),
        ]

    def keep_copy(self, p):
        return pltpu.make_async_copy(
            self.fin.at[:, self.lanes(p)], self.final_rows(p, 3), self.local.at[self.index + 16 * (p + 1)]
        )

    def spread(self, p, t):
        dp, me, _ = self.place
        return self.remote(
            self.fin.at[:, self.lanes(p)],
            self.final_rows(p, 3),
            11 + 3 * p + t - 1,
            (dp, lax.rem(me + t, 4)),
        )

    def doubling(self, p, depth):
        ref = self.final_rows(p, depth)
        return self.remote(ref, ref, 15 + 2 * (3 - depth) + p, self.partner(self.axes(p)[depth - 1]))

    def core_back(self):
        dp, me, bits = self.place
        ref = self.final_rows(None, 0)
        return self.remote(ref, ref, 21, (dp + 1 - 2 * bits[0], me))

    def add(self, first, buf, count, lanes):
        step = 128 if count % 128 == 0 else count

        def body(i):
            rows = self.rows(first + i * step, step)
            self.acc[rows, lanes] = self.acc[rows, lanes] + buf[pl.ds(pl.multiple_of(i * step, 16), step), lanes]

        loop(count // step, body)

    def stages(self):
        n = self.n
        both = range(len(self.parts))

        def s0():
            self.core_copy().start()
            self.own_copy().start()

        def s1():
            self.own_copy().wait()
            self.core_copy().wait()
            self.add(0, self.r0, n // 2, slice(None))
            for p in both:
                self.halving(p, 1).start()

        def s2():
            for p in both:
                self.halving(p, 1).wait()
                self.add(self.offset(p, 1), self.r1, n // 4, self.lanes(p))
                self.halving(p, 2).start()

        def s3():
            for p in both:
                self.halving(p, 2).wait()
                self.add(self.offset(p, 2), self.r2, n // 8, self.lanes(p))
                for t in range(1, 4):
                    self.quarter(p, t).start()

        def s4():
            for p in both:
                for t in range(1, 4):
                    self.quarter(p, t).wait()
                lanes = self.lanes(p)
                mine = self.acc[self.rows(self.offset(p, 3), n // 32), lanes].astype(f32)
                for t in range(3):
                    mine = mine + self.r3[t, :, lanes].astype(f32)
                self.fin[:, lanes] = mine.astype(bf)
                self.keep_copy(p).start()
                for t in range(1, 4):
                    self.spread(p, t).start()

        def s5():
            for p in both:
                self.keep_copy(p).wait()
                for t in range(1, 4):
                    self.spread(p, t).wait()
                self.doubling(p, 2).start()

        def s6():
            for p in both:
                self.doubling(p, 2).wait()
                self.doubling(p, 1).start()

        def s7():
            for p in both:
                self.doubling(p, 1).wait()
            self.core_back().start()

        def s8():
            self.core_back().wait()

        return [s0, s1, s2, s3, s4, s5, s6, s7, s8]


def seg_scratch(n, w):
    return [
        pltpu.VMEM((n // 2, w), bf),
        pltpu.VMEM((n // 2, w), bf),
        pltpu.VMEM((n // 4, w), bf),
        pltpu.VMEM((n // 8, w), bf),
        pltpu.VMEM((3, n // 32, w), bf),
        pltpu.VMEM((n // 32, w), bf),
    ]


SEGMENTS = [(FF, D), (FF + D, D), (4 * D, D)] + [(D, 384)] * PAIRS


def backward_kernel(
    x, packed, sh, qfs, kfs, n1, r1, q8, mem, kv, qfc, kfc, dfc, pre2, do, gffn, vecs_in,
    wqkv, wso, wcq, wckv, gain, bias, omega,
    igrad, mgrad, f1, f2, f3, vout,
    fl, qg, kvg, mgs, pre1, br1, dos, dfs, pg, g2, g3, vec, vbuf, vz,
    *rest,
):
    seg_bufs, (send, recv, local, vsend, vrecv, msend, mrecv) = rest[:-7], rest[-7:]
    me = lax.axis_index("mem")
    dp = lax.axis_index("dp")
    bits = (lax.rem(dp, 2), lax.rem(dp // 2, 2), lax.rem(dp // 4, 2))
    place = (dp, me, bits)
    near = [(dp + (1 << a) * (1 - 2 * bits[a]), me) for a in range(3)]
    peers = near + [(dp, lax.rem(me + t, 4)) for t in range(1, 4)]
    barrier = pltpu.get_barrier_semaphore()
    for peer in peers:
        pl.semaphore_signal(barrier, inc=1, device_id=peer, device_id_type=MESH)
    pl.semaphore_wait(barrier, len(peers))

    whole_parts = ((0, 256, 0), (256, 512, 1))
    pair_parts = ((0, 128, 0), (128, 384, 1))
    sources = [(gffn, 0), (gffn, FF), (g2, 0)] + [(g3.at[j], 0) for j in range(PAIRS)]
    finals = [(f1, 0), (f1, FF), (f2, 0)] + [(f3.at[j], 0) for j in range(PAIRS)]
    segs = []
    for i, (n, w) in enumerate(SEGMENTS):
        acc, b0, b1, b2, b3, fin = seg_bufs[6 * i : 6 * i + 6]
        parts = whole_parts if w == D else pair_parts
        segs.append(
            Segment(i, *sources[i], n, parts, acc, (b0, b1, b2, b3), fin, *finals[i], (send, recv, local), place).stages()
        )

    ticks = {}

    def at(phase, step, fn):
        ticks.setdefault((phase, step), []).append(fn)

    def run(phase, i):
        for (name, step), fns in ticks.items():
            if name == phase:

                @pl.when(i == step)
                def _(fns=fns):
                    for fn in fns:
                        fn()

    for k in range(9):
        at("cross", min(15, 2 * k), segs[0][k]) if k < 8 else None
        at("cross", 2 * k + 1, segs[1][k]) if k < 8 else None

    def first_low(i):
        rows = span(i, TB)
        fl[rows, :] = (n1[rows, :] * gain[0:1, :] + bias[0:1, :]).astype(bf)

    loop(L // TB, first_low)

    blocks = L // CROSS_BK

    def cross_pair(i):
        run("cross", i)
        j = i // blocks
        b = lax.rem(i, blocks)
        rows = span(b, CROSS_BK)
        lanes = span(j, 128)
        vlanes = pl.ds(pl.multiple_of(D + j * 128, 128), 128)
        k_rows = kv[rows, lanes]
        ka = jnp.concatenate([k_rows, kfc[rows, :]], axis=1)
        va = jnp.concatenate([kv[rows, vlanes], kfc[rows, :]], axis=1)
        dk, dv, dq = back_tile(
            ka, va, k_rows, q8[:, lanes], [qfc[2 * j], qfc[2 * j + 1]], do[:, lanes], [dfc[2 * j], dfc[2 * j + 1]], None
        )
        kvg[rows, lanes] = dk.astype(bf)
        kvg[rows, vlanes] = dv.astype(bf)

        @pl.when(b == 0)
        def _():
            pre1[:, lanes] = dq

        @pl.when(b > 0)
        def _():
            pre1[:, lanes] += dq

    loop(PAIRS * blocks, cross_pair)
    segs[0][8]()
    segs[1][8]()

    def query_low(i):
        rows = span(i, TB)
        qg[rows, :] = (pre1[rows, :] * SCALE).astype(bf)
        mgs[rows, :] = dot(kvg[rows, :], wckv[...], NT).astype(bf)

    loop(L // TB, query_low)

    def memory_back(t):
        peer = lax.rem(me + t, 4)
        return pltpu.make_async_remote_copy(
            src_ref=mgs.at[span(peer, L // 4), :],
            dst_ref=mgrad.at[me],
            send_sem=msend.at[t],
            recv_sem=mrecv.at[t],
            device_id=(dp, peer),
            device_id_type=MESH,
        )

    memory_own = pltpu.make_async_copy(mgs.at[span(me, L // 4), :], mgrad.at[me], msend.at[0])
    memory_own.start()
    for t in range(1, 4):
        memory_back(t).start()

    def weights_two(i):
        cols = span(i, 256)
        g2[cols, :] = dot(fl[:, cols], qg[...], TN).astype(bf)
        g2[pl.ds(pl.multiple_of(D + i * 256, 256), 256), :] = dot(mem[:, cols], kvg[:, :D], TN).astype(bf)
        g2[pl.ds(pl.multiple_of(2 * D + i * 256, 256), 256), :] = dot(mem[:, cols], kvg[:, D:], TN).astype(bf)

    loop(2, weights_two)
    vec[...] = jnp.zeros_like(vec)
    vec[0:9, :] = vecs_in[0:9, :]

    def first_back(i):
        rows = span(i, TB)
        normed = n1[rows, :]
        grad = omega[1:2, :] * pre2[rows, :] + dot(qg[rows, :], wcq[...], NT)
        back1 = norm_back(grad, normed, r1[rows, :], gain[0:1, :])
        vec[0:1, :] += total(grad * normed)
        vec[3:4, :] += total(grad)
        vec[6:7, :] += total(back1 * x[rows, :].astype(f32))
        pre1[rows, :] = back1
        low1 = back1.astype(bf)
        br1[rows, :] = low1
        dlow = dot(low1, wso[...], NT).astype(bf)
        dos[rows, :] = dlow

        def store(h, value):
            dfs[h, rows, :] = value

        delta_features(dlow.astype(f32) * sh[rows, :].astype(f32), store)

    loop(L // TB, first_back)

    def weights_out(i):
        cols = span(i, 256)
        g2[pl.ds(pl.multiple_of(3 * D + i * 256, 256), 256), :] = dot(sh[:, cols], br1[...], TN).astype(bf)

    loop(2, weights_out)

    def vec_near(a):
        return pltpu.make_async_remote_copy(
            src_ref=vec.at[pl.ds(16 * a, 16), :],
            dst_ref=vbuf.at[a],
            send_sem=vsend.at[a],
            recv_sem=vrecv.at[a],
            device_id=near[a],
            device_id_type=MESH,
        )

    def vec_far(t):
        return pltpu.make_async_remote_copy(
            src_ref=vec.at[pl.ds(48, 16), :],
            dst_ref=vz.at[me],
            send_sem=vsend.at[2 + t],
            recv_sem=vrecv.at[2 + t],
            device_id=(dp, lax.rem(me + t, 4)),
            device_id_type=MESH,
        )

    def v_start():
        vec_near(0).start()

    def v_next(a):
        vec_near(a).wait()
        vec[16 * (a + 1) : 16 * (a + 2), :] = vec[16 * a : 16 * (a + 1), :] + vbuf[a]
        if a < 2:
            vec_near(a + 1).start()
        else:
            for t in range(1, 4):
                vec_far(t).start()

    def v_last():
        for t in range(1, 4):
            vec_far(t).wait()
        vz[me] = vec[48:64, :]
        vout[...] = (vz[0] + vz[1]) + (vz[2] + vz[3])

    v_start()
    segs[2][0]()
    at("self", 0, segs[2][1])
    at("self", 0, lambda: v_next(0))
    at("self", 1, segs[2][2])
    at("self", 1, lambda: v_next(1))
    at("self", 2, segs[2][3])
    at("self", 2, lambda: v_next(2))
    at("self", 3, segs[2][4])
    at("self", 3, v_last)
    at("self", 1, segs[3][0])
    at("self", 2, segs[3][1])
    at("self", 2, segs[4][0])
    at("self", 3, segs[3][2])
    at("self", 3, segs[4][1])
    at("self", 3, segs[5][0])

    below = lax.broadcasted_iota(jnp.int32, (SELF_BK, SELF_BK), 1) >= lax.broadcasted_iota(
        jnp.int32, (SELF_BK, SELF_BK), 0
    )

    def self_pair(j):
        run("self", j)
        qlanes = span(j, 128)
        klanes = pl.ds(pl.multiple_of(D + j * 128, 128), 128)
        vlanes = pl.ds(pl.multiple_of(2 * D + j * 128, 128), 128)
        dqs = []
        for b in range(L // SELF_BK):
            low, high = b * SELF_BK, (b + 1) * SELF_BK
            k_rows = packed[low:high, klanes]
            ka = jnp.concatenate([k_rows, kfs[low:high, :]], axis=1)
            va = jnp.concatenate([packed[low:high, vlanes], kfs[low:high, :]], axis=1)
            dk, dv, dq = back_tile(
                ka,
                va,
                k_rows,
                packed[low:, qlanes],
                [qfs[2 * j, low:, :], qfs[2 * j + 1, low:, :]],
                dos[low:, qlanes],
                [dfs[2 * j, low:, :], dfs[2 * j + 1, low:, :]],
                below,
            )
            pg[low:high, klanes] = dk.astype(bf)
            pg[low:high, vlanes] = dv.astype(bf)
            for i in range(b, L // SELF_BK):
                piece = dq[(i - b) * SELF_BK : (i - b + 1) * SELF_BK, :]
                if b == 0:
                    dqs.append(piece)
                else:
                    dqs[i] = dqs[i] + piece
        for i, piece in enumerate(dqs):
            pg[i * SELF_BK : (i + 1) * SELF_BK, qlanes] = (piece * SCALE).astype(bf)
        for c in range(3):
            lanes = pl.ds(pl.multiple_of(c * D + j * 128, 128), 128)
            g3[j, :, c * 128 : (c + 1) * 128] = dot(x[...], pg[:, lanes], TN).astype(bf)

    loop(PAIRS, self_pair)
    segs[6][0]()

    def input_back(i):
        rows = span(i, TB)
        igrad[rows, :] = omega[0:1, :] * pre1[rows, :] + dot(pg[rows, :], wqkv[...], NT)

    loop(L // TB, input_back)
    memory_own.wait()
    for t in range(1, 4):
        memory_back(t).wait()
    for k in range(1, 9):
        if k + 4 < 9:
            segs[2][k + 4]()
        if k + 2 < 9:
            segs[3][k + 2]()
        if k + 1 < 9:
            segs[4][k + 1]()
        segs[5][k]()
        segs[6][k]()


VM = pl.BlockSpec(memory_space=pltpu.VMEM)
ANY = pl.BlockSpec(memory_space=pl.ANY)


def per_device(
    inputs, memory, cotangent, tgt_len, src_len,
    self_qkv, self_out, cross_query, cross_kv, cross_out, ffn_in, ffn_out, ln_gain, ln_bias, omega_scale, dp,
):
    x = inputs.reshape(L, D)
    me = lax.axis_index("mem")
    own_src = lax.dynamic_slice_in_dim(src_len, me, 1, 0)
    meta = jnp.pad(jnp.concatenate([tgt_len, own_src], axis=0), ((0, 6), (0, 112)))

    shape = jax.ShapeDtypeStruct
    fwd_out = [
        shape((L, D), bf),
        shape((L, 3 * D), bf),
        shape((L, D), bf),
        shape((HEADS, L, 128), bf),
        shape((L, 128), bf),
        shape((L, D), f32),
        shape((L, 1), f32),
        shape((L, D), bf),
        shape((L, D), bf),
        shape((L, 2 * D), bf),
        shape((HEADS, L, 128), bf),
        shape((L, 128), bf),
        shape((HEADS, L, 128), bf),
        shape((L, D), f32),
        shape((L, D), bf),
        shape((2 * FF + D, D), bf),
        shape((16, D), f32),
    ]
    fwd = pl.pallas_call(
        forward_kernel,
        out_shape=fwd_out,
        in_specs=[VM] * 14,
        out_specs=[VM] * len(fwd_out),
        scratch_shapes=[
            pltpu.VMEM((L, 128), bf),
            pltpu.VMEM((L, 1), f32),
            pltpu.VMEM((L, D), bf),
            pltpu.VMEM((L, FF), bf),
            pltpu.VMEM((L, FF), bf),
            pltpu.VMEM((L, D), bf),
            pltpu.VMEM((L, D), bf),
            pltpu.VMEM((L, D), bf),
            pltpu.VMEM((TB, FF), f32),
            pltpu.SemaphoreType.DMA((4,)),
            pltpu.SemaphoreType.DMA((4,)),
            pltpu.SemaphoreType.DMA,
        ],
        compiler_params=pltpu.CompilerParams(collective_id=0, has_side_effects=True, vmem_limit_bytes=62 << 20),
        name="forward",
    )(
        x, memory, cotangent.reshape(L, D), meta, self_qkv, self_out, cross_query, cross_kv, cross_out,
        ffn_in, ffn_out, ln_gain, ln_bias, omega_scale,
    )
    (output, packed, sh, qfs, kfs, n1, r1, q8, mem, kv, qfc, kfc, dfc, pre2, do, gffn, vecs) = fwd

    bwd_out = [
        shape((L, D), f32),
        shape((4, L // 4, D), bf),
        shape((2 * FF + D, D), bf),
        shape((4 * D, D), bf),
        shape((PAIRS, D, 384), bf),
        shape((16, D), f32),
    ]
    scratch = [
        pltpu.VMEM((L, D), bf),
        pltpu.VMEM((L, D), bf),
        pltpu.VMEM((L, 2 * D), bf),
        pltpu.VMEM((L, D), bf),
        pltpu.VMEM((L, D), f32),
        pltpu.VMEM((L, D), bf),
        pltpu.VMEM((L, D), bf),
        pltpu.VMEM((HEADS, L, 128), bf),
        pltpu.VMEM((L, 3 * D), bf),
        pltpu.VMEM((4 * D, D), bf),
        pltpu.VMEM((PAIRS, D, 384), bf),
        pltpu.VMEM((64, D), f32),
        pltpu.VMEM((3, 16, D), f32),
        pltpu.VMEM((4, 16, D), f32),
    ]
    for n, w in SEGMENTS:
        scratch += seg_scratch(n, w)
    count = len(SEGMENTS)
    scratch += [
        pltpu.SemaphoreType.DMA((count, 22)),
        pltpu.SemaphoreType.DMA((count, 22)),
        pltpu.SemaphoreType.DMA((48,)),
        pltpu.SemaphoreType.DMA((6,)),
        pltpu.SemaphoreType.DMA((6,)),
        pltpu.SemaphoreType.DMA((4,)),
        pltpu.SemaphoreType.DMA((4,)),
    ]
    igrad, mgrad, f1, f2, f3, small = pl.pallas_call(
        backward_kernel,
        out_shape=bwd_out,
        in_specs=[VM] * 15 + [ANY] + [VM] * 8,
        out_specs=[VM] + [ANY] * 4 + [VM],
        scratch_shapes=scratch,
        compiler_params=pltpu.CompilerParams(collective_id=1, has_side_effects=True, vmem_limit_bytes=63 << 20),
        name="backward",
    )(
        x, packed, sh, qfs, kfs, n1, r1, q8, mem, kv, qfc, kfc, dfc, pre2, do, gffn, vecs,
        self_qkv, self_out, cross_query, cross_kv, ln_gain, ln_bias, omega_scale,
    )

    blocks = dp // 8
    if blocks > 1:
        groups = [[i + 8 * b for b in range(blocks)] for i in range(8)]
        f1, f2, f3, small = lax.psum((f1, f2, f3, small), "dp", axis_index_groups=groups)

    def columns(stack, count):
        return stack.reshape(count, D, D).transpose(1, 0, 2).reshape(D, count * D).astype(f32)

    qkv_grad = f3.reshape(PAIRS, D, 3, 128).transpose(1, 2, 0, 3).reshape(D, 3 * D).astype(f32)
    return (
        output.reshape(1, L, D),
        igrad.reshape(1, L, D),
        mgrad.astype(f32),
        qkv_grad,
        f2[3 * D :].astype(f32),
        f2[:D].astype(f32),
        columns(f2[D : 3 * D], 2),
        f1[2 * FF :].astype(f32),
        columns(f1[FF : 2 * FF], FF // D),
        f1[:FF].astype(f32),
        small[0:3],
        small[3:6],
        small[6:9],
    )


def solution(mesh):
    rows = P(("dp", "mem"), None, None)
    return jax.shard_map(
        functools.partial(per_device, dp=mesh.shape["dp"]),
        mesh=mesh,
        in_specs=(rows, P("dp", "mem", None), rows, P(("dp", "mem"), None), P("dp", None)) + (P(),) * 10,
        out_specs=(rows, rows, P("dp", "mem", None)) + (P(),) * 10,
        check_vma=False,
    )
```

time: 1200 us -> 279 us (0.23)
  waiting for transfers between devices: 611 us -> 0 us
  matrix products: 285 us -> 0 us
  Pallas kernels: 0 us -> 249 us
  local copies, waits for them, and re-layouts: 122 us -> 21.1 us
  other arithmetic: 98.3 us -> 7.65 us
  blocking collectives: 42.8 us -> 0 us
  loops' own time: 15.6 us -> 0 us
  between operations: 15.8 us -> 0.74 us
    psum x3 -> x0, waiting for transfers between devices: 292 us -> none  [the longest x1 228 us: per_device(): lax.psum((self_qkv_weight, self_out_weight, cross_query_weight, cross_kv_...]
    dot_general x68 -> x0, matrix products: 285 us -> none  [the longest x16 84.1 us: block_scores(): jnp.einsum('qhd,khd->hqk', split_heads(queries), split_heads(key_rows), p...]
    pallas_call x0 -> x2, Pallas kernels: none -> 249 us  [the longest x1 163 us: per_device(): pl.pallas_call(backward_kernel, out_shape=bwd_out, in_specs=[VM] * 15 + [...]
    all_gather x2 -> x0, waiting for transfers between devices: 157 us -> none  [the longest x1 81.4 us: per_device(): grad_rows = lax.all_gather(heads_grad, 'mem', axis=0, tiled=True)]
    reduce_scatter x2 -> x0, waiting for transfers between devices: 129 us -> none  [the longest x1 74.5 us: per_device(): lax.psum_scatter(mixed_rows.reshape(amount, length, model_dim).astype(jnp...]
    psum x1 -> x0, blocking collectives: 42.8 us -> none  [per_device(): lax.psum((self_qkv_weight, self_out_weight, cross_query_weight, cross_kv_...]
    reduce_sum x26 -> x0, other arithmetic: 33.1 us -> none  [the longest x1 16 us: per_device(): cross_summed = lax.psum(jnp.sum(exponent, axis=-1), 'mem')]
    pmax x1 -> x0, waiting for transfers between devices: 32.6 us -> none  [per_device(): lax.pmax(jnp.max(scores, axis=-1).astype(jnp.bfloat16), 'mem')]
  transfers between devices with their start and end apart: 8 -> 0, of which waited for: 8 -> 0; matrix products, arithmetic and copies ran while one was open for 4% -> 0% of each run, Pallas kernels for 0% -> 0%
where the time goes in v1:
time: 279 us; the launch traced here: 278 us
  Pallas kernels  249 us (89%)
  local copies, waits for them, and re-layouts  21.1 us (8%)
  other arithmetic  7.65 us (3%)
    pallas_call x1, Pallas kernels, per_device(): pl.pallas_call(backward_kernel, out_shape=bwd_out, in_specs=[VM] * 15 + [...  163 us
    pallas_call x1, Pallas kernels, per_device(): pl.pallas_call(forward_kernel, out_shape=fwd_out, in_specs=[VM] * 14, out...  86 us
    unnamed x17, local copies, waits for them, and re-layouts  9.63 us

profile of v1, /device:TPU:0, one launch (start us, length us, event | category | flops | bytes accessed | tf_op | source)
XLA Modules:
  0.0 278.2 jit_solution(11961660132681920913)
XLA Ops:
  0.6 0.0 copy-start
  0.7 0.7 copy-done
  1.3 0.7 pad_add_fusion
  2.0 0.6 pad.4.meta
  2.6 86.0 %forward.1 = (bf16[1024,512]{1,0:T(8,128)(2,1)}, bf16[1024,1536]{1,0:T(8,128)(2,1)}, bf16[1024,512]{1,0:T(8,128)(2,1)}, bf16[8,1024,128]{2,1,0:T(8,128)(2,1)}, b...) custom-call(bf16[1024,512]{1,0:T(8,128)(2,1)} %bitcast.23, ...), custom_call_target="tpu_custom_call" | custom-call | tf_op jit(solution)/shard_map/forward/pallas_call | solution.py:841
  88.7 162.7 %backward.1 = (f32[1024,512]{1,0:T(8,128)}, bf16[4,256,512]{2,1,0:T(8,128)(2,1)}, bf16[4608,512]{1,0:T(8,128)(2,1)}, bf16[2048,512]{1,0:T(8,128)(2,1)}, bf16[4,512,384]{2,1,0:T(8,128)(2,1)}, /*index=5*/f32[16,512]{1,0:T(8,128)}) custom-call(bf16[1024,512]{1,0:T(8,128)(2,1)} %bitcast.24, bf16[1024,1536]{1,0:T(8,128)(2,1)} %get-tuple-element.37.packed, ...), custom_call_target="tpu_custom_call" | custom-call | tf_op jit(solution)/shard_map/backward/pallas_call | solution.py:904
  251.4 1.4 fusion
  252.8 1.3 slice.29
  254.1 0.0 copy-start.2
  254.1 0.3 convert_bitcast_fusion.1
  254.4 0.0 copy-start.4
  254.4 1.5 copy.39
  256.0 1.3 copy-done.2
  257.2 0.8 copy-done.4
  258.0 1.8 slice_convert_fusion.2
  259.8 2.7 slice_convert_fusion
  262.5 0.6 convert_bitcast_fusion
  263.1 0.0 copy-start.5
  263.1 2.7 copy.40
  265.8 0.0 copy-done.5
  265.8 1.6 convert_element_type.51
  267.4 1.7 copy.34
  269.1 2.2 copy.35
  271.3 0.0 copy-start.6
  271.3 3.6 %copy.38 = f32[512,1536]{1,0:T(8,128)} copy(f32[512,1536]{0,1:T(8,128)} %bitcast.21) | data formatting | bytes 6291456
  274.9 0.0 copy-done.6
  274.9 0.0 copy-start.3
  274.9 0.0 copy-start.1
  274.9 1.0 copy.43
  275.9 1.0 copy-done.3
  276.9 1.3 copy.44
  278.2 0.0 copy-done.1
  (1 shorter events, 0.0 us)
Async XLA Ops:
  0.6 0.7 copy-start
  254.1 3.1 %copy-start.2 = (bf16[4608,512]{1,0:T(8,128)(2,1)S(1)}, bf16[4608,512]{1,0:T(8,128)(2,1)}, u32[]{:S(2)}) copy-start(bf16[4608,512]{1,0:T(8,128)(2,1)} %get-tuple-element.57) | copy-start | bytes 14155780
  254.4 3.6 %copy-start.4 = (bf16[2048,512]{1,0:T(8,128)(2,1)S(1)}, bf16[2048,512]{1,0:T(8,128)(2,1)}, u32[]{:S(2)}) copy-start(bf16[2048,512]{1,0:T(8,128)(2,1)} %get-tuple-element.56) | copy-start | bytes 6291460
  263.1 2.7 copy-start.5
  271.3 3.6 %copy-start.6 = (bf16[1024,512]{1,0:T(8,128)(2,1)S(1)}, bf16[1024,512]{1,0:T(8,128)(2,1)}, u32[]{:S(2)}) copy-start(bf16[1024,512]{1,0:T(8,128)(2,1)} %get-tuple-element.36) | copy-start | bytes 3145732
  274.9 2.0 copy-start.3
  274.9 3.3 %copy-start.1 = (s32[4,16]{1,0:T(4,128)S(1)}, s32[4,16]{1,0:T(4,128)}, u32[]{:S(2)}) copy-start(s32[4,16]{1,0:T(4,128)} %param.19) | copy-start | bytes 772

commit v2 on v1

v2 whole, which is shorter than its diff:
```python
import functools

import jax
import jax.numpy as jnp
from jax import lax
from jax.experimental import pallas as pl
from jax.experimental.pallas import tpu as pltpu
from jax.sharding import PartitionSpec as P

f32 = jnp.float32
bf = jnp.bfloat16
MESH = pl.DeviceIdType.MESH
NN = (((1,), (0,)), ((), ()))
NT = (((1,), (1,)), ((), ()))
TN = (((0,), (0,)), ((), ()))

L = 1024
D = 512
FF = 2048
HEADS = 8
PAIRS = HEADS // 2
SHORT = 64
SCALE = 0.125
NEG = -1e30
EPS = 1e-05
GELU_C = 0.7978845608028654
GELU_A = 0.044715


def dot(a, b, dims=NN):
    return lax.dot_general(a, b, dims, preferred_element_type=f32)


def span(i, n):
    return pl.ds(pl.multiple_of(i * n, n), n)


def loop(n, body):
    def step(i, carry):
        body(i)
        return carry

    lax.fori_loop(0, n, step, 0)


def half_lanes():
    return lax.broadcasted_iota(jnp.int32, (1, 128), 1) < 64


def norm(values):
    centred = values - jnp.mean(values, axis=-1, keepdims=True)
    scaler = lax.rsqrt(jnp.mean(centred * centred, axis=-1, keepdims=True) + EPS)
    return centred * scaler, scaler


def norm_back(upstream, normed, scaler, gain_row):
    scaled = upstream * gain_row
    centred = scaled - jnp.mean(scaled, axis=-1, keepdims=True)
    centred = centred - normed * jnp.mean(scaled * normed, axis=-1, keepdims=True)
    return centred * scaler


def total(values):
    return jnp.sum(values, axis=0, keepdims=True)


def lane_of():
    return lax.broadcasted_iota(jnp.int32, (1, 128), 1)


def put_parts(values, head, old):
    at = lane_of() - (16 + 3 * head)
    high = values.astype(bf).astype(f32)
    rest = values - high
    middle = rest.astype(bf).astype(f32)
    low = rest - middle
    return jnp.where(at == 0, high, jnp.where(at == 1, middle, jnp.where(at == 2, low, old)))


def head_keys(feats, head):
    at = lane_of() - (16 + 3 * head)
    return jnp.where((at >= 0) & (at < 3), jnp.ones_like(feats), feats)


def key_features(lengths, is_doc, rows, first):
    pos = first + lax.broadcasted_iota(jnp.int32, (rows, 128), 0)
    lane = lax.broadcasted_iota(jnp.int32, (rows, 128), 1)
    seg = (pos >> 6) * (1 - is_doc)
    inside = (seg == lane) & (pos - seg * SHORT < lengths)
    feats = jnp.where(lane < 16, jnp.where(inside, 0.0, NEG), 0.0)
    hot = jnp.where(seg == lane, 1.0, 0.0)
    return feats.astype(bf), hot.astype(bf), jnp.where(inside, 1.0, 0.0)


def softmax_pair(j, qp, hot, sections, lse_ref, rows):
    half = half_lanes()
    mixed = []
    feats = lse_ref[rows, :].astype(f32)
    for e in range(2):
        sel = half if e == 0 else jnp.logical_not(half)
        qa = jnp.concatenate([jnp.where(sel, qp, jnp.zeros_like(qp)), hot], axis=1)
        scores = []
        largest = None
        for keys, _, mask in sections:
            s = dot(qa, keys, NT)
            if mask is not None:
                s = jnp.where(mask, s, NEG)
            scores.append(s)
            m = jnp.max(s, axis=1, keepdims=True)
            largest = m if largest is None else jnp.maximum(largest, m)
        acc = None
        for s, (_, values, _) in zip(scores, sections):
            o = dot(jnp.exp(s - largest).astype(bf), values)
            acc = o if acc is None else acc + o
        summed = acc[:, 128:]
        feats = put_parts(-(largest + jnp.log(summed)), 2 * j + e, feats)
        mixed.append(acc[:, :128] / summed)
    lse_ref[rows, :] = feats.astype(bf)
    return jnp.where(half, mixed[0], mixed[1]).astype(bf)


def back_tile(j, k_rows, v_rows, kfeat, qp, qfeat, gp, gfeat, mask):
    half = half_lanes()
    dk, dv, dq = [], [], []
    for e in range(2):
        sel = half if e == 0 else jnp.logical_not(half)
        kf = head_keys(kfeat, 2 * j + e)
        qa = jnp.concatenate([jnp.where(sel, qp, jnp.zeros_like(qp)), qfeat], axis=1)
        ga = jnp.concatenate([jnp.where(sel, gp, jnp.zeros_like(gp)), gfeat], axis=1)
        probs = jnp.exp(dot(jnp.concatenate([k_rows, kf], axis=1), qa, NT))
        if mask is not None:
            width = mask.shape[1]
            first = jnp.where(mask, probs[:, :width], 0.0)
            probs = first if probs.shape[1] == width else jnp.concatenate([first, probs[:, width:]], axis=1)
        ds = (probs * dot(jnp.concatenate([v_rows, kf], axis=1), ga, NT)).astype(bf)
        dv.append(dot(probs.astype(bf), gp))
        dk.append(dot(ds, qp))
        dq.append(dot(ds, k_rows, TN))
    return (
        jnp.where(half, dk[0], dk[1]),
        jnp.where(half, dv[0], dv[1]),
        jnp.where(half, dq[0], dq[1]),
    )


def delta_features(product):
    half = half_lanes()
    feats = jnp.zeros((product.shape[0], 128), f32)
    for j in range(PAIRS):
        part = product[:, 128 * j : 128 * (j + 1)]
        for e in range(2):
            sel = half if e == 0 else jnp.logical_not(half)
            delta = jnp.sum(jnp.where(sel, part, 0.0), axis=1, keepdims=True)
            feats = put_parts(-delta, 2 * j + e, feats)
    return feats.astype(bf)


SELF_BQ = 256
SELF_BK = 256
CROSS_BQ = 512
CROSS_BK = 256
TB = 256
WIDE = 512


class Segment:
    def __init__(self, index, source, parts, bufs, final, sems, place):
        self.index, self.source, self.parts = index, source, parts
        self.n = source.shape[0]
        (self.r0, self.r1, self.r2, self.r3, self.fin) = bufs
        self.final = final
        self.send, self.recv, self.local = sems
        self.place = place

    def remote(self, src, dst, k, device):
        return pltpu.make_async_remote_copy(
            src_ref=src,
            dst_ref=dst,
            send_sem=self.send.at[self.index, k],
            recv_sem=self.recv.at[self.index, k],
            device_id=device,
            device_id_type=MESH,
        )

    def mine(self, first, count):
        return pl.ds(pl.multiple_of(self.place[2][0] * (self.n // 2) + first, 16), count)

    def core_copy(self):
        n, (dp, me, bits) = self.n, self.place
        other = pl.ds(pl.multiple_of((1 - bits[0]) * (n // 2), 16), n // 2)
        return self.remote(self.source.at[other, :], self.r0, 0, (dp + 1 - 2 * bits[0], me))

    def partner(self, axis):
        dp, me, bits = self.place
        return (dp + 2 * axis * (1 - 2 * bits[axis]), me)

    def axes(self, p):
        return (1, 2) if self.parts[p][2] == 0 else (2, 1)

    def lanes(self, p):
        return slice(self.parts[p][0], self.parts[p][1])

    def offset(self, p, depth):
        if depth == 0:
            return 0
        n, (_, me, bits) = self.n, self.place
        one, two = self.axes(p)
        result = bits[one] * (n // 4)
        if depth > 1:
            result = result + bits[two] * (n // 8)
        if depth > 2:
            result = result + me * (n // 32)
        return result

    def halving(self, p, depth):
        n, (_, _, bits) = self.n, self.place
        axis = self.axes(p)[depth - 1]
        size = n // (4 if depth == 1 else 8)
        other = self.offset(p, depth - 1) + (1 - bits[axis]) * size
        buf = self.r1 if depth == 1 else self.r2
        return self.remote(
            self.source.at[self.mine(other, size), self.lanes(p)],
            buf.at[:, self.lanes(p)],
            2 * depth - 1 + p,
            self.partner(axis),
        )

    def quarter(self, p, t):
        n, (dp, me, _) = self.n, self.place
        peer = lax.rem(me + t, 4)
        return self.remote(
            self.source.at[self.mine(self.offset(p, 2) + peer * (n // 32), n // 32), self.lanes(p)],
            self.r3.at[t - 1, :, self.lanes(p)],
            5 + 3 * p + t - 1,
            (dp, peer),
        )

    def final_rows(self, p, depth):
        size = self.n // (2, 4, 8, 32)[depth]
        lanes = slice(None) if p is None else self.lanes(p)
        return self.final.at[self.mine(self.offset(p, depth), size), lanes]

    def keep_copy(self, p):
        return pltpu.make_async_copy(
            self.fin.at[:, self.lanes(p)], self.final_rows(p, 3), self.local.at[2 * self.index + p]
        )

    def spread(self, p, t):
        dp, me, _ = self.place
        return self.remote(
            self.fin.at[:, self.lanes(p)],
            self.final_rows(p, 3),
            11 + 3 * p + t - 1,
            (dp, lax.rem(me + t, 4)),
        )

    def doubling(self, p, depth):
        ref = self.final_rows(p, depth)
        return self.remote(ref, ref, 15 + 2 * (3 - depth) + p, self.partner(self.axes(p)[depth - 1]))

    def core_back(self):
        dp, me, bits = self.place
        ref = self.final_rows(None, 0)
        return self.remote(ref, ref, 21, (dp + 1 - 2 * bits[0], me))

    def add(self, first, buf, count, lanes):
        step = 128 if count % 128 == 0 else count

        def body(i):
            rows = self.mine(first + i * step, step)
            self.source[rows, lanes] = self.source[rows, lanes] + buf[pl.ds(pl.multiple_of(i * step, 16), step), lanes]

        if count == step:
            body(0)
        else:
            loop(count // step, body)

    def stages(self):
        n = self.n
        both = range(len(self.parts))

        def s0():
            self.core_copy().start()

        def s1():
            self.core_copy().wait()
            self.add(0, self.r0, n // 2, slice(None))
            for p in both:
                self.halving(p, 1).start()

        def s2():
            for p in both:
                self.halving(p, 1).wait()
                self.add(self.offset(p, 1), self.r1, n // 4, self.lanes(p))
                self.halving(p, 2).start()

        def s3():
            for p in both:
                self.halving(p, 2).wait()
                self.add(self.offset(p, 2), self.r2, n // 8, self.lanes(p))
                for t in range(1, 4):
                    self.quarter(p, t).start()

        def s4():
            for p in both:
                for t in range(1, 4):
                    self.quarter(p, t).wait()
                lanes = self.lanes(p)
                mine = self.source[self.mine(self.offset(p, 3), n // 32), lanes].astype(f32)
                for t in range(3):
                    mine = mine + self.r3[t, :, lanes].astype(f32)
                self.fin[:, lanes] = mine.astype(bf)
                self.keep_copy(p).start()
                for t in range(1, 4):
                    self.spread(p, t).start()

        def s5():
            for p in both:
                self.keep_copy(p).wait()
                for t in range(1, 4):
                    self.spread(p, t).wait()
                self.doubling(p, 2).start()

        def s6():
            for p in both:
                self.doubling(p, 2).wait()
                self.doubling(p, 1).start()

        def s7():
            for p in both:
                self.doubling(p, 1).wait()
            self.core_back().start()

        def s8():
            self.core_back().wait()

        return [s0, s1, s2, s3, s4, s5, s6, s7, s8]


SEGMENTS = [(FF, D), (D, FF), (4 * D, D), (D, D)] + [(D, 384)] * PAIRS


def seg_scratch(n, w):
    return [
        pltpu.VMEM((n // 2, w), bf),
        pltpu.VMEM((n // 4, w), bf),
        pltpu.VMEM((n // 8, w), bf),
        pltpu.VMEM((3, n // 32, w), bf),
        pltpu.VMEM((n // 32, w), bf),
    ]


SCHEDULE = {
    0: [("in_weight", 0), ("in_weight", 7), ("cross", 4), ("cross", 9), ("cross", 14), ("first", 1), ("self", 1), ("self", 8), ("self", 10)],
    1: [("cross", 0), ("cross", 3), ("cross", 7), ("cross", 10), ("query", 1), ("self", 0), ("self", 5), ("self", 13), ("input", 0)],
    2: [("first", 0), ("so", 0), ("self", 4), ("self", 10), ("self", 15), ("end", 2), ("end", 8), ("end", 15), ("end", 21)],
    3: [("self", 0), ("self", 1), ("self", 9), ("self", 13), ("input", 0), ("end", 3), ("end", 9), ("end", 16), ("end", 22)],
    4: [("self", 4), ("self", 5), ("self", 14), ("input", 1), ("end", 5), ("end", 11), ("end", 17), ("end", 23), ("end", 26)],
    5: [("self", 8), ("self", 11), ("self", 14), ("input", 1), ("end", 6), ("end", 12), ("end", 18), ("end", 24), ("end", 28)],
    6: [("self", 12), ("self", 15), ("input", 2), ("end", 1), ("end", 7), ("end", 13), ("end", 20), ("end", 27), ("end", 29)],
    7: [("input", 2), ("end", 0), ("end", 4), ("end", 10), ("end", 14), ("end", 19), ("end", 25), ("end", 30), ("end", 31)],
}


def layer_kernel(
    tgt_len, src_len, x_in, meml, cot_in, wqkv_in, wso_in, wcq_in, wckv_in, wco_in, win_in, wout_in, gain, bias, omega,
    out, igrad, mgrad, f_out, f_in, f_two, f_so, f_qkv, vout,
    x, cot, wqkv, wso, wcq, wckv, wco, win, wout,
    packed, sh, n1, r1, q8, mem, kv, ch, qfs, kfs, qfc, kfc, dfc, hot, keep, pre2, do,
    act, hg, br3, slow, br2, dg, g2, gso, g3, vec, vbuf, vz,
    *rest,
):
    (load_sem, out_sem, send, recv, local, vsend, vrecv, xsend, xrecv, msend, mrecv) = rest[-11:]
    seg_bufs = rest[:-11]
    me = lax.axis_index("mem")
    dp = lax.axis_index("dp")
    n = 4
    piece = L // n
    bits = (lax.rem(dp, 2), lax.rem(dp // 2, 2), lax.rem(dp // 4, 2))
    place = (dp, me, bits)
    near = [(dp + (1 << a) * (1 - 2 * bits[a]), me) for a in range(3)]
    peers = near + [(dp, lax.rem(me + t, n)) for t in range(1, n)]

    loads = {}
    for i, (name, src, dst) in enumerate(
        [
            ("x", x_in, x), ("wqkv", wqkv_in, wqkv), ("wso", wso_in, wso), ("wcq", wcq_in, wcq), ("wckv", wckv_in, wckv),
            ("wco", wco_in, wco), ("win", win_in, win), ("wout", wout_in, wout), ("cot", cot_in, cot),
        ]
    ):
        loads[name] = pltpu.make_async_copy(src, dst, load_sem.at[i])
        loads[name].start()

    barrier = pltpu.get_barrier_semaphore()
    for peer in peers:
        pl.semaphore_signal(barrier, inc=1, device_id=peer, device_id_type=MESH)
    pl.semaphore_wait(barrier, len(peers))

    def exchange(t):
        peer = lax.rem(me + t, n)
        return pltpu.make_async_remote_copy(
            src_ref=meml.at[peer],
            dst_ref=mem.at[span(me, piece), :],
            send_sem=xsend.at[t],
            recv_sem=xrecv.at[t],
            device_id=(dp, peer),
            device_id_type=MESH,
        )

    own = pltpu.make_async_copy(meml.at[me], mem.at[span(me, piece), :], xsend.at[0])
    for t in range(1, n):
        exchange(t).start()
    own.start()

    whole_parts = ((0, 256, 0), (256, 512, 1))
    wide_parts = ((0, 1024, 0), (1024, 2048, 1))
    pair_parts = ((0, 128, 0), (128, 384, 1))
    sources = [wout, win, g2, gso] + [g3.at[j] for j in range(PAIRS)]
    finals = [f_out, f_in, f_two, f_so] + [f_qkv.at[j] for j in range(PAIRS)]
    ticks = {}
    for i, (rows, width) in enumerate(SEGMENTS):
        parts = {D: whole_parts, FF: wide_parts, 384: pair_parts}[width]
        stages = Segment(i, sources[i], parts, seg_bufs[5 * i : 5 * i + 5], finals[i], (send, recv, local), place).stages()
        for (phase, step), fn in zip(SCHEDULE[i], stages):
            ticks.setdefault(phase, []).append((step, i, fn))

    def at(phase, step, fn):
        ticks.setdefault(phase, []).append((step, -1, fn))

    def run(phase, i, unit=1, part=0):
        todo = {}
        for step, order, fn in ticks.get(phase, []):
            if step % unit == part:
                todo.setdefault(step // unit, []).append((order, fn))
        for step, fns in sorted(todo.items()):

            @pl.when(i == step)
            def _(fns=fns):
                for _, fn in sorted(fns, key=lambda item: item[0]):
                    fn()

    lane = lane_of()
    lengths = [jnp.zeros((1, 128), jnp.int32)] * 2
    for s in range(16):
        lengths[0] = jnp.where(lane == s, tgt_len[0, s], lengths[0])
        lengths[1] = jnp.where(lane == s, src_len[me, s], lengths[1])
    is_doc = jnp.where(src_len[me, 0] > SHORT, 1, 0)

    def features(i):
        rows = span(i, TB)
        feats, one_hot, inside = key_features(lengths[0], is_doc, TB, i * TB)
        kfs[rows, :] = feats
        hot[rows, :] = one_hot
        qfs[rows, :] = one_hot
        qfc[rows, :] = one_hot
        keep[rows, :] = jnp.sum(inside, axis=1, keepdims=True)
        feats, _, _ = key_features(lengths[1], is_doc, TB, i * TB)
        kfc[rows, :] = feats

    loop(L // TB, features)
    loads["x"].wait()
    loads["wqkv"].wait()

    def project(i):
        rows = span(i, TB)
        packed[rows, :D] = dot(x[rows, :], wqkv[:, :D]).astype(bf) * bf(SCALE)
        packed[rows, D:] = dot(x[rows, :], wqkv[:, D:]).astype(bf)

    loop(L // TB, project)

    causal = lax.broadcasted_iota(jnp.int32, (SELF_BQ, SELF_BQ), 0) >= lax.broadcasted_iota(
        jnp.int32, (SELF_BQ, SELF_BQ), 1
    )

    def lanes_at(first, j):
        return pl.ds(pl.multiple_of(first + j * 128, 128), 128)

    for b in range(L // SELF_BQ):
        low, high = b * SELF_BQ, (b + 1) * SELF_BQ

        def self_pair(j, low=low, high=high):
            def section(first, last, mask):
                keys = jnp.concatenate([packed[first:last, lanes_at(D, j)], kfs[first:last, :]], axis=1)
                values = packed[first:last, lanes_at(2 * D, j)]
                return keys, jnp.concatenate([values, jnp.ones((last - first, 128), bf)], axis=1), mask

            sections = [section(low, high, causal)]
            if low:
                sections.append(section(0, low, None))
            sh[low:high, span(j, 128)] = softmax_pair(
                j, packed[low:high, span(j, 128)], hot[low:high, :], sections, qfs, slice(low, high)
            )

        loop(PAIRS, self_pair)

    loads["wso"].wait()
    loads["wcq"].wait()

    def first_norm(i):
        rows = span(i, TB)
        normed, scaler = norm(omega[0:1, :] * x[rows, :].astype(f32) + dot(sh[rows, :], wso[...]))
        n1[rows, :] = normed
        r1[rows, :] = scaler
        first = (normed * gain[0:1, :] + bias[0:1, :]).astype(bf)
        q8[rows, :] = dot(first, wcq[...]).astype(bf) * bf(SCALE)

    loop(L // TB, first_norm)

    own.wait()
    for t in range(1, n):
        exchange(t).wait()
    loads["wckv"].wait()

    def memory_project(i):
        rows = span(i, TB)
        kv[rows, :] = dot(mem[rows, :], wckv[...]).astype(bf)

    loop(L // TB, memory_project)

    def cross_pair(i):
        j = i // (L // CROSS_BQ)
        rows = span(lax.rem(i, L // CROSS_BQ), CROSS_BQ)
        keys = jnp.concatenate([kv[:, span(j, 128)], kfc[...]], axis=1)
        values = jnp.concatenate([kv[:, lanes_at(D, j)], jnp.ones((L, 128), bf)], axis=1)
        ch[rows, span(j, 128)] = softmax_pair(j, q8[rows, span(j, 128)], hot[rows, :], [(keys, values, None)], qfc, rows)

    loop(PAIRS * (L // CROSS_BQ), cross_pair)

    vec[...] = jnp.zeros_like(vec)
    for name in ("wco", "win", "wout", "cot"):
        loads[name].wait()

    def tokens(i):
        rows = span(i, TB)
        first = n1[rows, :] * gain[0:1, :] + bias[0:1, :]
        n2, r2 = norm(omega[1:2, :] * first + dot(ch[rows, :], wco[...]))
        second = n2 * gain[1:2, :] + bias[1:2, :]
        second_low = second.astype(bf)
        slow[rows, :] = second_low
        branch = jnp.zeros((TB, D), f32)
        for c in range(FF // WIDE):
            cols = slice(c * WIDE, (c + 1) * WIDE)
            h = dot(second_low, win[:, cols])
            square = h * h
            th = jnp.tanh(GELU_C * (h + GELU_A * (h * square)))
            cdf = 0.5 * (1.0 + th)
            low = (h * cdf).astype(bf)
            act[rows, cols] = low
            dg[c * TB : (c + 1) * TB, :] = cdf + 0.5 * h * (1.0 - th * th) * (GELU_C * (1.0 + 3.0 * GELU_A * square))
            branch = branch + dot(low, wout[cols, :])
        n3, r3 = norm(omega[2:3, :] * second + branch)
        third = n3 * gain[2:3, :] + bias[2:3, :]
        kept = keep[rows, :]
        up = cot[rows, :].astype(f32) * kept
        cot[rows, :] = (third * kept).astype(bf)
        pre3 = norm_back(up, n3, r3, gain[2:3, :])
        vec[2:3, :] += total(up * n3)
        vec[5:6, :] += total(up)
        vec[8:9, :] += total(pre3 * second)
        low3 = pre3.astype(bf)
        br3[rows, :] = low3
        grad = omega[2:3, :] * pre3
        for c in range(FF // WIDE):
            cols = slice(c * WIDE, (c + 1) * WIDE)
            hl = (dot(low3, wout[cols, :], NT) * dg[c * TB : (c + 1) * TB, :]).astype(bf)
            hg[rows, cols] = hl
            grad = grad + dot(hl, win[:, cols], NT)
        back2 = norm_back(grad, n2, r2, gain[1:2, :])
        vec[1:2, :] += total(grad * n2)
        vec[4:5, :] += total(grad)
        vec[7:8, :] += total(back2 * first)
        pre2[rows, :] = back2
        low2 = back2.astype(bf)
        br2[rows, :] = low2
        dlow = dot(low2, wco[...], NT).astype(bf)
        do[rows, :] = dlow
        dfc[rows, :] = delta_features(dlow.astype(f32) * ch[rows, :].astype(f32))

    loop(L // TB, tokens)
    out_copy = pltpu.make_async_copy(cot, out, out_sem.at[0])
    out_copy.start()

    def out_weight(i):
        wout[span(i, 256), :] = dot(act[:, span(i, 256)], br3[...], TN).astype(bf)

    loop(FF // 256, out_weight)

    def in_weight(i):
        run("in_weight", i)
        rows = span(i // 4, 256)
        cols = span(lax.rem(i, 4), WIDE)
        win[rows, cols] = dot(slow[:, rows], hg[:, cols], TN).astype(bf)

    loop(8, in_weight)

    def cross_out_weight(i):
        run("co", i)
        g2[span(i, 256), :] = dot(ch[:, span(i, 256)], br2[...], TN).astype(bf)

    loop(2, cross_out_weight)

    kvg, qg, fl = hg.at[:, : 2 * D], hg.at[:, 2 * D : 3 * D], hg.at[:, 3 * D :]
    pg, mgs = act.at[:, : 3 * D], act.at[:, 3 * D :]
    pre1, br1 = dg, br3
    blocks = L // CROSS_BK

    def cross_back(i):
        run("cross", i)
        j = i // blocks
        b = lax.rem(i, blocks)
        rows = span(b, CROSS_BK)
        lanes = span(j, 128)
        dk, dv, dq = back_tile(
            j, kv[rows, lanes], kv[rows, lanes_at(D, j)], kfc[rows, :], q8[:, lanes], qfc[...], do[:, lanes], dfc[...], None
        )
        kvg[rows, lanes] = dk.astype(bf)
        kvg[rows, lanes_at(D, j)] = dv.astype(bf)

        @pl.when(b == 0)
        def _():
            pre1[:, lanes] = dq

        @pl.when(b > 0)
        def _():
            pre1[:, lanes] += dq

    loop(PAIRS * blocks, cross_back)

    def query_low(i):
        run("query", i)
        rows = span(i, TB)
        fl[rows, :] = (n1[rows, :] * gain[0:1, :] + bias[0:1, :]).astype(bf)
        qg[rows, :] = (pre1[rows, :] * SCALE).astype(bf)
        mgs[rows, :] = dot(kvg[rows, :], wckv[...], NT).astype(bf)

    loop(L // TB, query_low)

    def memory_back(t):
        peer = lax.rem(me + t, n)
        return pltpu.make_async_remote_copy(
            src_ref=mgs.at[span(peer, piece), :],
            dst_ref=mgrad.at[me],
            send_sem=msend.at[t],
            recv_sem=mrecv.at[t],
            device_id=(dp, peer),
            device_id_type=MESH,
        )

    memory_own = pltpu.make_async_copy(mgs.at[span(me, piece), :], mgrad.at[me], msend.at[0])
    memory_own.start()
    for t in range(1, n):
        memory_back(t).start()

    def weights_two(i):
        run("two", i)
        cols = span(i, 256)
        g2[pl.ds(pl.multiple_of(D + i * 256, 256), 256), :] = dot(fl[:, cols], qg[...], TN).astype(bf)
        g2[pl.ds(pl.multiple_of(2 * D + i * 256, 256), 256), :] = dot(mem[:, cols], kvg[:, :D], TN).astype(bf)
        g2[pl.ds(pl.multiple_of(3 * D + i * 256, 256), 256), :] = dot(mem[:, cols], kvg[:, D:], TN).astype(bf)

    loop(2, weights_two)

    def first_back(i):
        run("first", i)
        rows = span(i, TB)
        normed = n1[rows, :]
        grad = omega[1:2, :] * pre2[rows, :] + dot(qg[rows, :], wcq[...], NT)
        back1 = norm_back(grad, normed, r1[rows, :], gain[0:1, :])
        vec[0:1, :] += total(grad * normed)
        vec[3:4, :] += total(grad)
        vec[6:7, :] += total(back1 * x[rows, :].astype(f32))
        pre1[rows, :] = back1
        low1 = back1.astype(bf)
        br1[rows, :] = low1
        dlow = dot(low1, wso[...], NT).astype(bf)
        do[rows, :] = dlow
        dfc[rows, :] = delta_features(dlow.astype(f32) * sh[rows, :].astype(f32))

    loop(L // TB, first_back)

    def self_out_weight(i):
        run("so", i)
        gso[span(i, 256), :] = dot(sh[:, span(i, 256)], br1[...], TN).astype(bf)

    loop(2, self_out_weight)

    def vec_near(a):
        return pltpu.make_async_remote_copy(
            src_ref=vec.at[pl.ds(16 * a, 16), :],
            dst_ref=vbuf.at[a],
            send_sem=vsend.at[a],
            recv_sem=vrecv.at[a],
            device_id=near[a],
            device_id_type=MESH,
        )

    def vec_far(t):
        return pltpu.make_async_remote_copy(
            src_ref=vec.at[pl.ds(48, 16), :],
            dst_ref=vz.at[me],
            send_sem=vsend.at[2 + t],
            recv_sem=vrecv.at[2 + t],
            device_id=(dp, lax.rem(me + t, n)),
            device_id_type=MESH,
        )

    def vec_next(a):
        vec_near(a).wait()
        vec[16 * (a + 1) : 16 * (a + 2), :] = vec[16 * a : 16 * (a + 1), :] + vbuf[a]
        if a < 2:
            vec_near(a + 1).start()
        else:
            for t in range(1, n):
                vec_far(t).start()

    def vec_last():
        for t in range(1, n):
            vec_far(t).wait()
        vz[me] = vec[48:64, :]
        vout[...] = (vz[0] + vz[1]) + (vz[2] + vz[3])

    vec_near(0).start()
    at("self", 1, lambda: vec_next(0))
    at("self", 3, lambda: vec_next(1))
    at("self", 5, lambda: vec_next(2))
    at("self", 8, vec_last)

    below = lax.broadcasted_iota(jnp.int32, (SELF_BK, SELF_BK), 1) >= lax.broadcasted_iota(
        jnp.int32, (SELF_BK, SELF_BK), 0
    )
    parts = L // SELF_BK

    def self_back(j):
        dqs = []
        for b in range(parts):
            run("self", j, parts, b)
            low, high = b * SELF_BK, (b + 1) * SELF_BK
            dk, dv, dq = back_tile(
                j,
                packed[low:high, lanes_at(D, j)],
                packed[low:high, lanes_at(2 * D, j)],
                kfs[low:high, :],
                packed[low:, span(j, 128)],
                qfs[low:, :],
                do[low:, span(j, 128)],
                dfc[low:, :],
                below,
            )
            pg[low:high, lanes_at(D, j)] = dk.astype(bf)
            pg[low:high, lanes_at(2 * D, j)] = dv.astype(bf)
            for i in range(b, parts):
                share = dq[(i - b) * SELF_BK : (i - b + 1) * SELF_BK, :]
                if b == 0:
                    dqs.append(share)
                else:
                    dqs[i] = dqs[i] + share
        for i, share in enumerate(dqs):
            pg[i * SELF_BK : (i + 1) * SELF_BK, span(j, 128)] = (share * SCALE).astype(bf)
        for c in range(3):
            g3[j, :, c * 128 : (c + 1) * 128] = dot(x[...], pg[:, lanes_at(c * D, j)], TN).astype(bf)

    loop(PAIRS, self_back)

    def igrad_copy(i):
        return pltpu.make_async_copy(pre1.at[span(i, TB), :], igrad.at[span(i, TB), :], out_sem.at[1 + i])

    def input_back(i):
        run("input", i)
        rows = span(i, TB)
        pre1[rows, :] = omega[0:1, :] * pre1[rows, :] + dot(pg[rows, :], wqkv[...], NT)
        igrad_copy(i).start()

    loop(L // TB, input_back)
    out_copy.wait()
    memory_own.wait()
    for t in range(1, n):
        memory_back(t).wait()
    for _, _, fn in sorted(ticks["end"], key=lambda item: item[:2]):
        fn()
    for i in range(L // TB):
        igrad_copy(i).wait()


CASTS = (
    [(0, (slice(i * D, (i + 1) * D), slice(0, D)), 0, (slice(i * D, (i + 1) * D), slice(0, D))) for i in range(4)]
    + [(1, (slice(0, D), slice(i * D, (i + 1) * D)), 1, (slice(0, D), slice(i * D, (i + 1) * D))) for i in range(4)]
    + [
        (2, (slice(0, D), slice(0, D)), 2, (slice(0, D), slice(0, D))),
        (2, (slice(D, 2 * D), slice(0, D)), 3, (slice(0, D), slice(0, D))),
        (2, (slice(2 * D, 3 * D), slice(0, D)), 4, (slice(0, D), slice(0, D))),
        (2, (slice(3 * D, 4 * D), slice(0, D)), 4, (slice(0, D), slice(D, 2 * D))),
        (3, (slice(0, D), slice(0, D)), 5, (slice(0, D), slice(0, D))),
    ]
)


def cast_kernel(
    out_in, igrad_in, mgrad_in, f_out, f_in, f_two, f_so, f_qkv,
    out, igrad, mgrad, g_out, g_in, g_co, g_cq, g_ckv, g_so, g_qkv,
    narrow, wide, qkv_narrow, qkv_wide, out_held, igrad_held, sems, out_sems,
):
    passed = [(out_in, out_held, out), (igrad_in, igrad_held, igrad)]
    whole_in = [pltpu.make_async_copy(src, held, sems.at[i]) for i, (src, held, _) in enumerate(passed)]
    froms = (f_out, f_in, f_two, f_so)
    tos = (g_out, g_in, g_co, g_cq, g_ckv, g_so)
    pieces = []
    for source, window, target, place in CASTS:
        pieces.append((froms[source].at[window], tos[target].at[place]))
    for i in range(2):
        pieces.append((mgrad_in.at[pl.ds(i * D, D), :], mgrad.at[pl.ds(i * D, D), :]))
    ins = [pltpu.make_async_copy(src, narrow.at[i], sems.at[2 + i]) for i, (src, _) in enumerate(pieces)]
    outs = [pltpu.make_async_copy(wide.at[i], dst, out_sems.at[i]) for i, (_, dst) in enumerate(pieces)]
    qkv_in = pltpu.make_async_copy(f_qkv, qkv_narrow, sems.at[2 + len(pieces)])
    qkv_out = pltpu.make_async_copy(qkv_wide, g_qkv, out_sems.at[len(pieces)])
    for copy in ins:
        copy.start()
    qkv_in.start()
    whole_out = [
        pltpu.make_async_copy(held, dst, out_sems.at[len(pieces) + 1 + i]) for i, (_, held, dst) in enumerate(passed)
    ]
    for copy in whole_in:
        copy.start()
    for i, copy in enumerate(ins):
        copy.wait()

        def body(r, i=i):
            wide[i, span(r, 64), :] = narrow[i, span(r, 64), :].astype(f32)

        loop(D // 64, body)
        outs[i].start()
    qkv_in.wait()

    def body(r):
        for j in range(PAIRS):
            for c in range(3):
                qkv_wide[span(r, 64), c * D + j * 128 : c * D + (j + 1) * 128] = qkv_narrow[
                    j, span(r, 64), c * 128 : (c + 1) * 128
                ].astype(f32)

    loop(D // 64, body)
    qkv_out.start()
    for copy_in, copy_out in zip(whole_in, whole_out):
        copy_in.wait()
        copy_out.start()
    for copy in whole_out + outs:
        copy.wait()
    qkv_out.wait()


VM = pl.BlockSpec(memory_space=pltpu.VMEM)
SM = pl.BlockSpec(memory_space=pltpu.SMEM)
ANY = pl.BlockSpec(memory_space=pl.ANY)


def per_device(
    inputs, memory, cotangent, tgt_len, src_len,
    self_qkv, self_out, cross_query, cross_kv, cross_out, ffn_in, ffn_out, ln_gain, ln_bias, omega_scale, dp,
):
    shape = jax.ShapeDtypeStruct
    scratch = [
        pltpu.VMEM((L, D), bf),
        pltpu.VMEM((L, D), bf),
        pltpu.VMEM((D, 3 * D), bf),
        pltpu.VMEM((D, D), bf),
        pltpu.VMEM((D, D), bf),
        pltpu.VMEM((D, 2 * D), bf),
        pltpu.VMEM((D, D), bf),
        pltpu.VMEM((D, FF), bf),
        pltpu.VMEM((FF, D), bf),
        pltpu.VMEM((L, 3 * D), bf),
        pltpu.VMEM((L, D), bf),
        pltpu.VMEM((L, D), f32),
        pltpu.VMEM((L, 1), f32),
        pltpu.VMEM((L, D), bf),
        pltpu.VMEM((L, D), bf),
        pltpu.VMEM((L, 2 * D), bf),
        pltpu.VMEM((L, D), bf),
        pltpu.VMEM((L, 128), bf),
        pltpu.VMEM((L, 128), bf),
        pltpu.VMEM((L, 128), bf),
        pltpu.VMEM((L, 128), bf),
        pltpu.VMEM((L, 128), bf),
        pltpu.VMEM((L, 128), bf),
        pltpu.VMEM((L, 1), f32),
        pltpu.VMEM((L, D), f32),
        pltpu.VMEM((L, D), bf),
        pltpu.VMEM((L, FF), bf),
        pltpu.VMEM((L, FF), bf),
        pltpu.VMEM((L, D), bf),
        pltpu.VMEM((L, D), bf),
        pltpu.VMEM((L, D), bf),
        pltpu.VMEM((L, D), f32),
        pltpu.VMEM((4 * D, D), bf),
        pltpu.VMEM((D, D), bf),
        pltpu.VMEM((PAIRS, D, 384), bf),
        pltpu.VMEM((64, D), f32),
        pltpu.VMEM((3, 16, D), f32),
        pltpu.VMEM((4, 16, D), f32),
    ]
    for n, w in SEGMENTS:
        scratch += seg_scratch(n, w)
    count = len(SEGMENTS)
    sem = pltpu.SemaphoreType.DMA
    scratch += [
        sem((9,)), sem((5,)), sem((count, 22)), sem((count, 22)), sem((2 * count,)), sem((6,)), sem((6,)),
        sem((4,)), sem((4,)), sem((4,)), sem((4,)),
    ]
    results = pl.pallas_call(
        layer_kernel,
        out_shape=[
            shape((L, D), bf),
            shape((L, D), f32),
            shape((4, L // 4, D), bf),
            shape((FF, D), bf),
            shape((D, FF), bf),
            shape((4 * D, D), bf),
            shape((D, D), bf),
            shape((PAIRS, D, 384), bf),
            shape((16, D), f32),
        ],
        in_specs=[SM] * 2 + [ANY] * 10 + [VM] * 3,
        out_specs=[ANY] * 8 + [VM],
        scratch_shapes=scratch,
        compiler_params=pltpu.CompilerParams(collective_id=0, has_side_effects=True, vmem_limit_bytes=63 << 20),
        name="layer",
    )(
        tgt_len, src_len, inputs.reshape(L, D), memory, cotangent.reshape(L, D), self_qkv, self_out, cross_query, cross_kv,
        cross_out, ffn_in, ffn_out, ln_gain, ln_bias, omega_scale,
    )
    output, igrad, mgrad, grads, small = results[0], results[1], results[2], results[3:8], results[8]

    blocks = dp // 8
    if blocks > 1:
        groups = [[i + 8 * b for b in range(blocks)] for i in range(8)]
        *grads, small = lax.psum((*grads, small), "dp", axis_index_groups=groups)

    pieces = len(CASTS) + 2
    output, igrad, mgrad, g_out, g_in, g_co, g_cq, g_ckv, g_so, g_qkv = pl.pallas_call(
        cast_kernel,
        out_shape=[
            shape((L, D), bf),
            shape((L, D), f32),
            shape((L, D), f32),
            shape((FF, D), f32),
            shape((D, FF), f32),
            shape((D, D), f32),
            shape((D, D), f32),
            shape((D, 2 * D), f32),
            shape((D, D), f32),
            shape((D, 3 * D), f32),
        ],
        in_specs=[ANY] * 8,
        out_specs=[ANY] * 10,
        scratch_shapes=[
            pltpu.VMEM((pieces, D, D), bf),
            pltpu.VMEM((pieces, D, D), f32),
            pltpu.VMEM((PAIRS, D, 384), bf),
            pltpu.VMEM((D, 3 * D), f32),
            pltpu.VMEM((L, D), bf),
            pltpu.VMEM((L, D), f32),
            sem((pieces + 3,)),
            sem((pieces + 3,)),
        ],
        compiler_params=pltpu.CompilerParams(vmem_limit_bytes=62 << 20),
        name="casts",
    )(output, igrad, mgrad.reshape(L, D), *grads)
    return (
        output.reshape(1, L, D),
        igrad.reshape(1, L, D),
        mgrad.reshape(4, L // 4, D),
        g_qkv,
        g_so,
        g_cq,
        g_ckv,
        g_co,
        g_in,
        g_out,
        small[0:3],
        small[3:6],
        small[6:9],
    )


def solution(mesh):
    rows = P(("dp", "mem"), None, None)
    return jax.shard_map(
        functools.partial(per_device, dp=mesh.shape["dp"]),
        mesh=mesh,
        in_specs=(rows, P("dp", "mem", None), rows, P(("dp", "mem"), None), P("dp", None)) + (P(),) * 10,
        out_specs=(rows, rows, P("dp", "mem", None)) + (P(),) * 10,
        check_vma=False,
    )
```

time: 279 us -> 216 us (0.77)
  Pallas kernels: 249 us -> 212 us
  local copies, waits for them, and re-layouts: 21.1 us -> 1.45 us
  other arithmetic: 7.65 us -> 0 us
    pallas_call x2, Pallas kernels: 249 us -> 212 us  [the longest x1 199 us: per_device(): pl.pallas_call(layer_kernel, out_shape=[shape((L, D), bf), shape((L, D),...]
    unnamed x17 -> x0, local copies, waits for them, and re-layouts: 9.63 us -> none
    convert_element_type x4 -> x0, local copies, waits for them, and re-layouts: 8.1 us -> none  [the longest x2 4.19 us: columns(): stack.reshape(count, D, D).transpose(1, 0, 2).reshape(D, count * D)]
    convert_element_type x3 -> x0, other arithmetic: 6.14 us -> none  [the longest x1 2.73 us: per_device(): f1[:FF].astype(f32)]
where the time goes in v2:
time: 216 us; the launch traced here: 214 us
  Pallas kernels  212 us (98%)
    pallas_call x1, Pallas kernels, per_device(): pl.pallas_call(layer_kernel, out_shape=[shape((L, D), bf), shape((L, D),...  199 us
    pallas_call x1, Pallas kernels, per_device(): pl.pallas_call(cast_kernel, out_shape=[shape((L, D), bf), shape((L, D), f...  12.4 us

profile of v2, /device:TPU:0, one launch (start us, length us, event | category | flops | bytes accessed | tf_op | source)
XLA Modules:
  0.0 213.9 jit_solution(173333235318552276)
XLA Ops:
  0.7 199.3 %layer.1 = (bf16[1024,512]{1,0:T(8,128)(2,1)}, f32[1024,512]{1,0:T(8,128)}, bf16[4,256,512]{2,1,0:T(8,128)(2,1)}, bf16[2048,512]{1,0:T(8,128)(2,1)}, bf16[512,20...) custom-call(s32[1,16]{1,0:T(1,128)} %tgt_len.1, ...), custom_call_target="tpu_custom_call" | custom-call | tf_op jit(solution)/shard_map/layer/pallas_call | solution.py:908
  199.9 1.4 fusion
  201.4 12.4 %casts.1 = (bf16[1024,512]{1,0:T(8,128)(2,1)}, f32[1024,512]{1,0:T(8,128)}, f32[1024,512]{1,0:T(8,128)}, f32[2048,512]{1,0:T(8,128)}, f32[512,2048]{1,0:T(8,128)...) custom-call(bf16[1024,512]{1,0:T(8,128)(2,1)} %get-tuple-element.32., ...), custom_call_target="tpu_custom_call" | custom-call | tf_op jit(solution)/shard_map/casts/pallas_call | solution.py:938
